TPU v7x, 128 devices: a whole 4x4x4 slice. The times are simulated.
128 devices in a mesh: pair: 8 (over z, core), virt: 16 (over y, x).
Axes of the slice: x: 4, y: 4, z: 4, core: 2. Of those that a mesh axis runs over, the one named last changes fastest.
Arguments:
- amplitudes: bfloat16 [64, 2048, 2048], P('pair', 'virt'), may hold values from -6 to 6
- cycle_panel: bfloat16 [2048, 2048], P(('pair', 'virt')), may hold values from -0.125 to 0.125
- ladder_panel: bfloat16 [2048, 2048], P(('pair', 'virt')), may hold values from -0.125 to 0.125
- virt_energy: float32 [2048], replicated, may hold values from 0.5 to 8
- pair_energy: float32 [64], P('pair'), may hold values from -4 to -1
- tile_mask: int32 [64, 32, 32], P('pair', None, 'virt'), may hold values 0 or 1
Outputs:
- updated: bfloat16 [64, 2048, 2048], P('pair', None, 'virt')
All inputs are finite; a program needn't handle non-finite values. No bound on the sum of `tile_mask` on one device may be relied on, other than what follows from the above.
Results may differ from a plain program's by a relative error of at most 0.004.
Values may be sent and summed in bfloat16 or wider, within the bound.
No kernel may reach another device: no remote copies, remote signals or barrier semaphores. Data moves between devices by JAX's collectives and lax.ppermute only.
A program may use at most 128 MiB of HBM per device.

v0:
```python
import jax
import jax.numpy as jnp
from jax import lax
from jax.sharding import PartitionSpec as P

TILE = 64


def local(amplitudes, cycle_panel, ladder_panel, virt_energy, pair_energy, tile_mask):
    pair_count = amplitudes.shape[0]
    virt_width = amplitudes.shape[2]
    full_cycle, full_ladder = (
        lax.all_gather(cycle_panel, ("pair", "virt"), axis=0, tiled=True),
        lax.all_gather(ladder_panel, ("pair", "virt"), axis=0, tiled=True),
    )
    half_ladder = jnp.einsum(
        "rad,bd->rab", amplitudes, full_ladder, preferred_element_type=jnp.float32
    ).astype(jnp.bfloat16)
    amps_virt = lax.all_to_all(amplitudes, "virt", split_axis=2, concat_axis=1, tiled=True)
    half_virt = lax.all_to_all(half_ladder, "virt", split_axis=2, concat_axis=1, tiled=True)
    result = jnp.einsum("ac,rcb->rab", full_cycle, amps_virt, preferred_element_type=jnp.float32)
    combined = result + jnp.einsum(
        "ac,rcb->rab", full_ladder, half_virt, preferred_element_type=jnp.float32
    )
    column_width = combined.shape[2]
    tiles_all = virt_width // TILE
    tiles_local = column_width // TILE
    screen = tile_mask.astype(jnp.float32)[:, :, None, :, None]
    masked = combined.reshape(pair_count, tiles_all, TILE, tiles_local, TILE) * screen
    column_start = lax.axis_index("virt") * column_width
    column_energy = lax.dynamic_slice_in_dim(virt_energy, column_start, column_width)
    denominator = (
        virt_energy[None, :, None] + column_energy[None, None, :] - pair_energy[:, None, None]
    )
    return (masked.reshape(pair_count, virt_width, column_width) / denominator).astype(jnp.bfloat16)


def solution(mesh):
    in_specs = (
        P("pair", "virt", None),
        P(("pair", "virt"), None),
        P(("pair", "virt"), None),
        P(),
        P("pair"),
        P("pair", None, "virt"),
    )
    out_specs = P("pair", None, "virt")
    return jax.shard_map(local, mesh=mesh, in_specs=in_specs, out_specs=out_specs, check_vma=False)
```

profile of v0, /device:TPU:1, one launch (start us, length us, event | category | flops | bytes accessed | tf_op | source)
XLA Modules:
  0.0 273.8 jit_solution(17230344357012899102)
XLA Ops:
  6.5 0.0 all-gather.5.cloned.1.call-start
  6.5 0.7 all-gather.5.cloned.1.call-update
  7.3 0.0 all-gather.3.cloned.1.call-start
  7.3 0.7 all-gather.3.cloned.1.call-update
  8.0 6.8 %copy.10 = bf16[8,128,2048]{1,0,2:T(8,128)(2,1)} copy(bf16[8,128,2048]{2,1,0:T(8,128)(2,1)} %param.6) | data formatting | bytes 8388608 | tf_op args[0]
  14.8 7.6 %all-to-all-start = ((bf16[8,128,2048]{1,0,2:T(8,128)(2,1)}), bf16[8,128,2048]{1,0,2:T(8,128)(2,1)}, u32[]{:S(2)}, u32[]{:S(2)}) async-start(bf16[8,128,2048]{1,0,2:T(8,128)(2,1)} %copy.10), calls=%async_computation | async-start | bytes 8388608 | tf_op jit(solution)/shard_map/all_to_all | solution.py:19
  22.4 100.1 %all-gather.5.cloned.1.call-done = bf16[2048,2048]{1,0:T(8,128)(2,1)} async-done(((bf16[16,2048]{1,0:T(8,128)(2,1)}), bf16[2048,2048]{1,0:T(8,128)(2,1)}) %all-gather.5.cloned.1.call-update) | async-done | bytes 8388624 | tf_op jit(solution)/shard_map/all_gather | solution.py:14
  122.5 13.9 %fusion.10 = bf16[8,128,2048]{2,1,0:T(8,128)(2,1)} fusion(bf16[8,128,2048]{2,1,0:T(8,128)(2,1)} %param.6, bf16[2048,2048]{1,0:T(8,128)(2,1)} %all-gather.5.cloned.1.call-done), kind=kOutput, calls=%fused_computation.11 | convolution fusion | flops 8592031744 | bytes 16777216 | tf_op jit(solution)/shard_map/rad,bd->rab/dot_general | solution.py:16
  136.4 6.8 %copy.12 = bf16[8,128,2048]{1,0,2:T(8,128)(2,1)} copy(bf16[8,128,2048]{2,1,0:T(8,128)(2,1)} %fusion.10) | data formatting | bytes 8388608 | tf_op jit(solution)/shard_map/convert_element_type | solution.py:18
  143.1 0.0 all-to-all-done
  143.1 4.7 %all-to-all-start.1 = ((bf16[8,128,2048]{1,0,2:T(8,128)(2,1)}), bf16[8,128,2048]{1,0,2:T(8,128)(2,1)}, u32[]{:S(2)}, u32[]{:S(2)}) async-start(bf16[8,128,2048]{1,0,2:T(8,128)(2,1)} %copy.12), calls=%async_computation.1 | async-start | bytes 8388608 | tf_op jit(solution)/shard_map/all_to_all | solution.py:20
  147.9 8.0 %mul.14 = f32[8,32,64,2,64]{2,1,4,3,0:T(8,128)} broadcast(f32[8,32,2]{1,2,0:T(2,128)S(1)} %convert_element_type.10), dimensions={0,1,3} | broadcast | bytes 8390656 | tf_op jit(solution)/shard_map/mul | solution.py:29
  155.9 14.9 %mul.15 = f32[8,2048,128]{1,2,0:T(8,128)} reshape(f32[8,32,64,2,64]{2,1,4,3,0:T(8,128)} %mul.14) | data formatting | bytes 16777216 | tf_op jit(solution)/shard_map/mul | solution.py:29
  170.7 0.0 copy-done
  170.7 0.1 dynamic_slice.3
  170.8 0.1 broadcast_add_fusion
  170.9 6.9 %copy.18 = bf16[8,128,16,128]{1,2,3,0:T(8,128)(2,1)} copy(bf16[8,128,16,128]{1,0,3,2:T(8,128)(2,1)} %bitcast) | data formatting | bytes 8388608 | tf_op jit(solution)/shard_map/all_to_all | solution.py:19
  177.8 7.3 %all_to_all.29 = bf16[8,2048,128]{1,2,0:T(8,128)(2,1)} reshape(bf16[8,16,128,128]{2,1,3,0:T(8,128)(2,1)} %bitcast.41) | data formatting | bytes 8388608 | tf_op jit(solution)/shard_map/all_to_all | solution.py:19
  185.1 28.3 %all-to-all-done.1 = bf16[8,128,2048]{1,0,2:T(8,128)(2,1)} async-done(((bf16[8,128,2048]{1,0,2:T(8,128)(2,1)}), bf16[8,128,2048]{1,0,2:T(8,128)(2,1)}, u32[]{:S(2)}, u32[]{:S(2)}) %all-to-all-start.1) | async-done | bytes 4194336 | tf_op jit(solution)/shard_map/all_to_all | solution.py:20
  213.5 6.9 %copy.17 = bf16[8,128,16,128]{1,2,3,0:T(8,128)(2,1)} copy(bf16[8,128,16,128]{1,0,3,2:T(8,128)(2,1)} %bitcast.4) | data formatting | bytes 8388608 | tf_op jit(solution)/shard_map/all_to_all | solution.py:20
  220.4 7.4 %all_to_all.33 = bf16[8,2048,128]{1,2,0:T(8,128)(2,1)} reshape(bf16[8,16,128,128]{2,1,3,0:T(8,128)(2,1)} %bitcast.42) | data formatting | bytes 8388608 | tf_op jit(solution)/shard_map/all_to_all | solution.py:20
  227.8 14.7 %fusion.2 = f32[8,128,2048]{2,1,0:T(8,128)} fusion(bf16[8,2048,128]{1,2,0:T(8,128)(2,1)} %all_to_all.33, bf16[2048,2048]{1,0:T(8,128)(2,1)} %all-gather.5.cloned.1.call-done), kind=kOutput, calls=%fused_computation.3 | convolution fusion | flops 8589934592 | bytes 20971520 | tf_op jit(solution)/shard_map/ac,rcb->rab/dot_general | solution.py:22
  242.5 18.1 %fusion.1 = bf16[8,2048,128]{1,2,0:T(8,128)(2,1)} fusion(f32[8,2048,128]{1,2,0:T(8,128)} %mul.15, f32[8,128,2048]{2,1,0:T(8,128)} %fusion.2, f32[8]{0:T(128)S(1)} %copy-done.2, f32[2048,128]{0,1:T(8,128)S(1)} %broadcast_add_fusion, bf16[8,2048,128]{1,2,0:T(8,128)(2,1)} %all_to_all.29, bf16[2048,2048]{1,0:T(8,128)(2,1)} %all-gather.3.cloned.1.call-done), kind=kOutput, calls=%fused_computation.2 | convolution fusion | flops 8600420352 | bytes 34603040 | tf_op jit(solution)/shard_map/ac,rcb->rab/dot_general | solution.py:21
  260.6 6.4 %copy.14 = bf16[8,2048,128]{2,1,0:T(8,128)(2,1)} copy(bf16[8,2048,128]{1,2,0:T(8,128)(2,1)} %fusion.1) | data formatting | bytes 8388608 | tf_op jit(solution)/shard_map/convert_element_type | solution.py:35
  (7 shorter events, 0.0 us)
Async XLA Ops:
  6.5 116.0 %all-gather.5.cloned.1.call-start = ((), (), s32[]{:S(2)}) async-start(), calls=%async_computation.3 | async-start | bytes 8454144 | tf_op jit(solution)/shard_map/all_gather | solution.py:14
  7.3 235.2 %all-gather.3.cloned.1.call-start = ((), (), s32[]{:S(2)}) async-start(), calls=%async_computation.2 | async-start | bytes 8454144 | tf_op jit(solution)/shard_map/all_gather | solution.py:13
  14.8 128.3 %all-to-all-start = ((bf16[8,128,2048]{1,0,2:T(8,128)(2,1)}), bf16[8,128,2048]{1,0,2:T(8,128)(2,1)}, u32[]{:S(2)}, u32[]{:S(2)}) async-start(bf16[8,128,2048]{1,0,2:T(8,128)(2,1)} %copy.10), calls=%async_computation | async-start | bytes 8388608 | tf_op jit(solution)/shard_map/all_to_all | solution.py:19
  136.4 11.5 %copy-start.1 = (s32[8,32,2]{1,2,0:T(2,128)S(1)}, s32[8,32,2]{1,2,0:T(2,128)}, u32[]{:S(2)}) copy-start(s32[8,32,2]{1,2,0:T(2,128)} %param.11) | copy-start | bytes 6148
  143.1 70.3 %all-to-all-start.1 = ((bf16[8,128,2048]{1,0,2:T(8,128)(2,1)}), bf16[8,128,2048]{1,0,2:T(8,128)(2,1)}, u32[]{:S(2)}, u32[]{:S(2)}) async-start(bf16[8,128,2048]{1,0,2:T(8,128)(2,1)} %copy.12), calls=%async_computation.1 | async-start | bytes 8388608 | tf_op jit(solution)/shard_map/all_to_all | solution.py:20
  155.9 14.9 %copy-start = (f32[2048]{0:T(1024)S(1)}, f32[2048]{0:T(1024)}, u32[]{:S(2)}) copy-start(f32[2048]{0:T(1024)} %param.9) | copy-start | bytes 24580
  227.8 14.7 %copy-start.2 = (f32[8]{0:T(128)S(1)}, f32[8]{0:T(128)}, u32[]{:S(2)}) copy-start(f32[8]{0:T(128)} %param.10) | copy-start | bytes 100
Sparse Core Ops, SparseCore 0:
  10.5 111.9 all-gather.4
  125.6 105.4 all-gather.2
where the time goes:
time: 275 us; the launch traced here: 274 us
  waiting for transfers between devices  130 us (47%)
  local copies, waits for them, and re-layouts  71.4 us (26%)
  matrix products  46.6 us (17%)
  between operations  13.5 us (5%)
  starting transfers between devices  12.4 us (5%)
    all_gather x1, waiting for transfers between devices, local(): lax.all_gather(ladder_panel, ('pair', 'virt'), axis=0, tiled=True)  100 us
    all_to_all x1, waiting for transfers between devices, local(): lax.all_to_all(half_ladder, 'virt', split_axis=2, concat_axis=1, tiled=True)  28.3 us
    mul x2, local copies, waits for them, and re-layouts, local(): combined.reshape(pair_count, tiles_all, TILE, tiles_local, TILE) * screen  22.8 us
    dot_general x1, matrix products, local(): jnp.einsum('ac,rcb->rab', full_cycle, amps_virt, preferred_element_type=j...  18.1 us
    dot_general x1, matrix products, local(): jnp.einsum('ac,rcb->rab', full_ladder, half_virt, preferred_element_type=...  14.7 us
    all_to_all x2, local copies, waits for them, and re-layouts, local(): lax.all_to_all(half_ladder, 'virt', split_axis=2, concat_axis=1, tiled=True)  14.3 us
    all_to_all x2, local copies, waits for them, and re-layouts, local(): lax.all_to_all(amplitudes, 'virt', split_axis=2, concat_axis=1, tiled=True)  14.2 us
    dot_general x1, matrix products, local(): jnp.einsum('rad,bd->rab', amplitudes, full_ladder, preferred_element_type...  13.9 us
  transfers between devices with their start and end apart: 4, of which 2 were waited for; matrix products, arithmetic and copies ran while one was open for 29% of the time, Pallas kernels for 0%

commit v1 on v0

v1 whole, which is shorter than its diff:
```python
import functools

import jax
import jax.numpy as jnp
from jax import lax
from jax.experimental import pallas as pl
from jax.experimental.pallas import tpu as pltpu
from jax.sharding import PartitionSpec as P

TILE = 64
LANES = 128
CHUNKS = 2
MIB = 1024 * 1024


def params(mib):
    return pltpu.CompilerParams(vmem_limit_bytes=mib * MIB)


def split_kernel(a_ref, out_ref):
    for k in range(out_ref.shape[0]):
        out_ref[k] = a_ref[:, :, k * LANES : (k + 1) * LANES]


def split_columns(amplitudes):
    pairs, rows, columns = amplitudes.shape
    owners = columns // LANES
    group = pairs // 2
    return pl.pallas_call(
        split_kernel,
        grid=(pairs // group,),
        in_specs=[pl.BlockSpec((group, rows, columns), lambda i: (i, 0, 0))],
        out_specs=pl.BlockSpec((owners, group, rows, LANES), lambda i: (0, i, 0, 0)),
        out_shape=jax.ShapeDtypeStruct((owners, pairs, rows, LANES), amplitudes.dtype),
        compiler_params=params(12),
        cost_estimate=pl.CostEstimate(flops=0, bytes_accessed=amplitudes.size * 4, transcendentals=0),
        name="split_columns",
    )(amplitudes)


def half_kernel(a_ref, l_ref, out_ref):
    pairs, rows, depth = a_ref.shape
    block = lax.dot_general(
        a_ref[...].reshape(pairs * rows, depth),
        l_ref[...],
        (((1,), (1,)), ((), ())),
        preferred_element_type=jnp.float32,
    ).astype(jnp.bfloat16)
    for k in range(out_ref.shape[0]):
        out_ref[k] = block[:, k * LANES : (k + 1) * LANES].reshape(pairs, rows, LANES)


def half_ladder(amplitudes, ladder, first, count):
    rows, depth = amplitudes.shape[1:]
    width = 512
    owners = ladder.shape[0] // LANES
    group = width // LANES
    return pl.pallas_call(
        half_kernel,
        grid=(ladder.shape[0] // width,),
        in_specs=[
            pl.BlockSpec((count, rows, depth), lambda i: (first // count, 0, 0)),
            pl.BlockSpec((width, depth), lambda i: (i, 0)),
        ],
        out_specs=pl.BlockSpec((group, count, rows, LANES), lambda i: (i, 0, 0, 0)),
        out_shape=jax.ShapeDtypeStruct((owners, count, rows, LANES), jnp.bfloat16),
        compiler_params=params(16),
        cost_estimate=pl.CostEstimate(
            flops=2 * count * rows * depth * ladder.shape[0],
            bytes_accessed=ladder.size * 2 + count * rows * depth * 4,
            transcendentals=0,
        ),
        name="half_ladder",
    )(amplitudes, ladder)


def widen(source, target):
    owners, count, rows, _ = source.shape
    for q in range(count // 2):
        for side in range(2):
            target[q, :, side * LANES : (side + 1) * LANES] = source[:, 2 * q + side].reshape(
                owners * rows, LANES
            )


def finish(first, total, q, energy_ref, base_ref, screen_ref, out_ref):
    height = total.shape[0]
    for side in range(2):
        r = 2 * q + side
        screen = jnp.broadcast_to(
            screen_ref[r][:, None, :], (height // TILE, TILE, LANES)
        ).reshape(height, LANES)
        masked = total[:, side * LANES : (side + 1) * LANES] * screen
        out_ref[r] = (masked / (base_ref[...] - energy_ref[first + r])).astype(out_ref.dtype)


def whole_kernel(first, energy_ref, k_ref, l_ref, a_ref, h_ref, base_ref, screen_ref, out_ref, a_wide, h_wide):
    @pl.when(pl.program_id(0) == 0)
    def _():
        widen(a_ref, a_wide)
        widen(h_ref, h_wide)

    for q in range(a_wide.shape[0]):
        total = jnp.dot(k_ref[...], a_wide[q], preferred_element_type=jnp.float32)
        total += jnp.dot(l_ref[...], h_wide[q], preferred_element_type=jnp.float32)
        finish(first, total, q, energy_ref, base_ref, screen_ref, out_ref)


def cycle_kernel(k_ref, a_ref, out_ref, a_wide):
    @pl.when(pl.program_id(0) == 0)
    def _():
        widen(a_ref, a_wide)

    for q in range(a_wide.shape[0]):
        out_ref[q] = jnp.dot(k_ref[...], a_wide[q], preferred_element_type=jnp.float32)


def ladder_kernel(first, energy_ref, l_ref, h_ref, part_ref, base_ref, screen_ref, previous_ref, out_ref, h_wide):
    del previous_ref

    @pl.when(pl.program_id(0) == 0)
    def _():
        widen(h_ref, h_wide)

    for q in range(h_wide.shape[0]):
        total = part_ref[q] + jnp.dot(l_ref[...], h_wide[q], preferred_element_type=jnp.float32)
        finish(first, total, q, energy_ref, base_ref, screen_ref, out_ref)


HEIGHT = 512


def specs(owners, count, rows, group):
    virt = owners * rows
    return dict(
        panel=pl.BlockSpec((HEIGHT, virt), lambda i: (i, 0)),
        amps=pl.BlockSpec((owners, count, rows, LANES), lambda i: (0, group, 0, 0)),
        half=pl.BlockSpec((owners, count, rows, LANES), lambda i: (0, 0, 0, 0)),
        part=pl.BlockSpec((count // 2, HEIGHT, 2 * LANES), lambda i: (0, i, 0)),
        base=pl.BlockSpec((HEIGHT, LANES), lambda i: (i, 0)),
        screen=pl.BlockSpec((count, HEIGHT // TILE, LANES), lambda i: (group, i, 0)),
        out=pl.BlockSpec((count, HEIGHT, LANES), lambda i: (group, i, 0)),
        energy=pl.BlockSpec(memory_space=pltpu.SMEM),
        wide=pltpu.VMEM((count // 2, virt, 2 * LANES), jnp.bfloat16),
    )


def cost(products, count, virt):
    return pl.CostEstimate(
        flops=2 * products * count * virt * virt * LANES,
        bytes_accessed=products * virt * virt * 2 + count * virt * LANES * 6,
        transcendentals=0,
    )


def update_whole(pair_energy, cycle, ladder, amps, half, base, screen, first):
    owners, count, rows, _ = half.shape
    virt = owners * rows
    at = specs(owners, count, rows, first // count)
    return pl.pallas_call(
        functools.partial(whole_kernel, first),
        grid=(virt // HEIGHT,),
        in_specs=[at[k] for k in ("energy", "panel", "panel", "amps", "half", "base", "screen")],
        out_specs=at["out"],
        out_shape=jax.ShapeDtypeStruct((amps.shape[1], virt, LANES), jnp.bfloat16),
        scratch_shapes=[at["wide"]] * 2,
        compiler_params=params(28),
        cost_estimate=cost(2, count, virt),
        name="update_whole",
    )(pair_energy, cycle, ladder, amps, half, base, screen)


def cycle_part(cycle, amps, first, count):
    owners, _, rows, _ = amps.shape
    virt = owners * rows
    at = specs(owners, count, rows, first // count)
    return pl.pallas_call(
        cycle_kernel,
        grid=(virt // HEIGHT,),
        in_specs=[at["panel"], at["amps"]],
        out_specs=at["part"],
        out_shape=jax.ShapeDtypeStruct((count // 2, virt, 2 * LANES), jnp.float32),
        scratch_shapes=[at["wide"]],
        compiler_params=params(20),
        cost_estimate=cost(1, count, virt),
        name="cycle_part",
    )(cycle, amps)


def update_ladder(pair_energy, ladder, half, part, base, screen, previous, first):
    owners, count, rows, _ = half.shape
    virt = owners * rows
    at = specs(owners, count, rows, first // count)
    return pl.pallas_call(
        functools.partial(ladder_kernel, first),
        grid=(virt // HEIGHT,),
        in_specs=[at[k] for k in ("energy", "panel", "half", "part", "base", "screen")]
        + [pl.BlockSpec(memory_space=pl.ANY)],
        out_specs=at["out"],
        out_shape=jax.ShapeDtypeStruct(previous.shape, previous.dtype),
        scratch_shapes=[at["wide"]],
        input_output_aliases={6: 0},
        compiler_params=params(24),
        cost_estimate=cost(1, count, virt),
        name="update_ladder",
    )(pair_energy, ladder, half, part, base, screen, previous)


def local(amplitudes, cycle_panel, ladder_panel, virt_energy, pair_energy, tile_mask):
    pairs = amplitudes.shape[0]
    count = pairs // CHUNKS
    exchange = functools.partial(
        lax.all_to_all, axis_name="virt", split_axis=0, concat_axis=0, tiled=True
    )
    gather = functools.partial(lax.all_gather, axis_name="pair", axis=0, tiled=True)
    after = lax.optimization_barrier
    with jax.named_scope("spread_panels"):
        rows, columns = ladder_panel.shape
        owners = columns // LANES
        both = jnp.concatenate([ladder_panel, cycle_panel])
        both = exchange(jnp.broadcast_to(both[None], (owners, 2 * rows, columns)))
        ladder_plane = both[:, :rows].reshape(owners * rows, columns)
        cycle_plane = both[:, rows:].reshape(owners * rows, columns)
    with jax.named_scope("gather_ladder"):
        ladder = gather(ladder_plane)
    with jax.named_scope("exchange_amplitudes"):
        own, _ = after((amplitudes, ladder_plane))
        amps = exchange(split_columns(own))
        own, cycle_plane, amps = after((own, cycle_plane, amps))
    with jax.named_scope("gather_cycle"):
        cycle = gather(cycle_plane)
    halves = []
    for chunk in range(CHUNKS):
        with jax.named_scope("half_ladder"):
            halves.append(exchange(half_ladder(own, ladder, chunk * count, count)))
    with jax.named_scope("update"):
        virt_energy, tile_mask, _ = after((virt_energy, tile_mask, halves[0]))
        column_start = lax.axis_index("virt") * LANES
        column_energy = lax.dynamic_slice_in_dim(virt_energy, column_start, LANES)
        base = virt_energy[:, None] + column_energy[None, :]
        screen = jnp.repeat(tile_mask.astype(jnp.float32), TILE, axis=2)
        out = update_whole(pair_energy, cycle, ladder, amps, halves[0], base, screen, 0)
        part = cycle_part(cycle, amps, count, count)
        return update_ladder(pair_energy, ladder, halves[1], part, base, screen, out, count)


def solution(mesh):
    in_specs = (
        P("pair", "virt", None),
        P(("pair", "virt"), None),
        P(("pair", "virt"), None),
        P(),
        P("pair"),
        P("pair", None, "virt"),
    )
    out_specs = P("pair", None, "virt")
    return jax.shard_map(local, mesh=mesh, in_specs=in_specs, out_specs=out_specs, check_vma=False)
```

time: 275 us -> 201 us (0.73)
  waiting for transfers between devices: 130 us -> 13.3 us
  blocking collectives: 0 us -> 87.9 us
  matrix products: 46.6 us -> 0 us
  Pallas kernels: 0 us -> 35.8 us
  local copies, waits for them, and re-layouts: 71.4 us -> 36.4 us
    all_gather x2, waiting for transfers between devices: 100 us -> 0.04 us  [the longest x1 0.02 us: local(): cycle = gather(cycle_plane)]
    all_to_all x0 -> x2, blocking collectives: none -> 87.9 us  [the longest x1 53.2 us: local(): amps = exchange(split_columns(own))]
    dot_general x3 -> x0, matrix products: 46.6 us -> none  [the longest x1 18.1 us: local(): jnp.einsum('ac,rcb->rab', full_cycle, amps_virt, preferred_element_type=j...]
    pallas_call x0 -> x6, Pallas kernels: none -> 35.8 us  [the longest x1 11.5 us: update_whole(): pl.pallas_call(functools.partial(whole_kernel, first), grid=(virt // HEIG...]
    all_to_all x4 -> x0, local copies, waits for them, and re-layouts: 28.5 us -> none  [the longest x2 14.3 us: local(): lax.all_to_all(half_ladder, 'virt', split_axis=2, concat_axis=1, tiled=True)]
    unnamed x7 -> x40, local copies, waits for them, and re-layouts: 6.8 us -> 34 us
    mul x2 -> x0, local copies, waits for them, and re-layouts: 22.8 us -> none  [local(): combined.reshape(pair_count, tiles_all, TILE, tiles_local, TILE) * screen]
    all_to_all x2, waiting for transfers between devices: 28.3 us -> 13.2 us  [local(): halves.append(exchange(half_ladder(own, ladder, chunk * count, count)))]
  transfers between devices with their start and end apart: 4 -> 4, of which waited for: 2 -> 1; matrix products, arithmetic and copies ran while one was open for 29% -> 1% of each run, Pallas kernels for 0% -> 14%
where the time goes in v1:
time: 201 us; the launch traced here: 200 us
  blocking collectives  87.9 us (44%)
  local copies, waits for them, and re-layouts  36.4 us (18%)
  Pallas kernels  35.8 us (18%)
  between operations  13.6 us (7%)
  waiting for transfers between devices  13.3 us (7%)
  starting transfers between devices  11.5 us (6%)
    all_to_all x1, blocking collectives, local(): amps = exchange(split_columns(own))  53.2 us
    all_to_all x1, blocking collectives, local(): both = exchange(jnp.broadcast_to(both[None], (owners, 2 * rows, columns)))  34.7 us
    unnamed x40, local copies, waits for them, and re-layouts  34 us
    all_to_all x2, waiting for transfers between devices, local(): halves.append(exchange(half_ladder(own, ladder, chunk * count, count)))  13.2 us
    pallas_call x1, Pallas kernels, update_whole(): pl.pallas_call(functools.partial(whole_kernel, first), grid=(virt // HEIG...  11.5 us
    all_to_all x2, starting transfers between devices, local(): halves.append(exchange(half_ladder(own, ladder, chunk * count, count)))  11.4 us
    pallas_call x2, Pallas kernels, half_ladder(): pl.pallas_call(half_kernel, grid=(ladder.shape[0] // width,), in_specs=[p...  10.3 us
    pallas_call x1, Pallas kernels, update_ladder(): pl.pallas_call(functools.partial(ladder_kernel, first), grid=(virt // HEI...  7.14 us
  transfers between devices with their start and end apart: 4, of which 1 were waited for; matrix products, arithmetic and copies ran while one was open for 1% of the time, Pallas kernels for 14%

profile of v1, /device:TPU:1, one launch (start us, length us, event | category | flops | bytes accessed | tf_op | source)
XLA Modules:
  0.0 199.7 jit_solution(7591724347306355388)
XLA Ops:
  7.7 34.7 %all_to_all.20 = bf16[16,32,2048]{2,1,0:T(8,128)(2,1)S(1)} all-to-all(bf16[16,32,2048]{2,1,0:T(8,128)(2,1)S(1)} %broadcast_in_dim.4), channel_id=1, replica_groups=mesh['pair'=8,'virt'=16] {'virt'}, dimensions={0} | all-to-all | bytes 4194304 | tf_op jit(solution)/shard_map/spread_panels/all_to_all | solution.py:221
  42.4 1.5 fusion
  44.0 2.2 %copy-done.10 = bf16[8,128,2048]{2,1,0:T(8,128)(2,1)S(1)} copy-done((bf16[8,128,2048]{2,1,0:T(8,128)(2,1)S(1)}, bf16[8,128,2048]{2,1,0:T(8,128)(2,1)}, u32[]{:S(2)}) %copy-start.10) | copy-done | bytes 4194328
  47.2 53.2 %all_to_all.21.a_ref = bf16[16,8,128,128]{3,2,1,0:T(8,128)(2,1)} all-to-all(bf16[16,8,128,128]{3,2,1,0:T(8,128)(2,1)S(1)} %split_columns.1), channel_id=1, replica_groups=mesh['pair'=8,'virt'=16] {'virt'}, dimensions={0} | all-to-all | bytes 8388608 | tf_op jit(solution)/shard_map/exchange_amplitudes/all_to_all | solution.py:228
  100.4 3.4 %copy-done.4 = bf16[2048,2048]{1,0:T(8,128)(2,1)S(1)} copy-done((bf16[2048,2048]{1,0:T(8,128)(2,1)S(1)}, bf16[2048,2048]{1,0:T(8,128)(2,1)}, u32[]{:S(2)}) %copy-start.4) | copy-done | bytes 8388632
  103.8 2.2 %copy-done.11 = bf16[8,128,2048]{2,1,0:T(8,128)(2,1)S(1)} copy-done((bf16[8,128,2048]{2,1,0:T(8,128)(2,1)S(1)}, bf16[8,128,2048]{2,1,0:T(8,128)(2,1)}, u32[]{:S(2)}) %copy-start.11) | copy-done | bytes 4194328
  106.0 5.2 %half_ladder.3 = bf16[16,4,128,128]{3,2,1,0:T(8,128)(2,1)S(1)} custom-call(bf16[8,128,2048]{2,1,0:T(8,128)(2,1)S(1)} %copy-done.11, bf16[2048,2048]{1,0:T(8,128)(2,1)S(1)} %copy-done.4), custom_call_target="tpu_custom_call" | custom-call | flops 4294967296 | bytes 12582912 | tf_op jit(solution)/shard_map/half_ladder/half_ladder/pallas_call | solution.py:58
  112.5 3.7 %all-to-all-start.3 = ((bf16[16,4,128,128]{3,2,1,0:T(8,128)(2,1)}), bf16[16,4,128,128]{3,2,1,0:T(8,128)(2,1)S(1)}, u32[]{:S(2)}, u32[]{:S(2)}) async-start(bf16[16,4,128,128]{3,2,1,0:T(8,128)(2,1)} %copy-done.16), calls=%async_computation.3 | async-start | bytes 4194304 | tf_op jit(solution)/shard_map/half_ladder/all_to_all | solution.py:235
  116.2 3.5 %copy-done.5 = bf16[2048,2048]{1,0:T(8,128)(2,1)S(1)} copy-done((bf16[2048,2048]{1,0:T(8,128)(2,1)S(1)}, bf16[2048,2048]{1,0:T(8,128)(2,1)}, u32[]{:S(2)}) %copy-start.5) | copy-done | bytes 8388632
  119.7 2.2 %copy-done.12 = bf16[8,128,2048]{2,1,0:T(8,128)(2,1)S(1)} copy-done((bf16[8,128,2048]{2,1,0:T(8,128)(2,1)S(1)}, bf16[8,128,2048]{2,1,0:T(8,128)(2,1)}, u32[]{:S(2)}) %copy-start.12) | copy-done | bytes 4194328
  121.9 5.2 %half_ladder.2 = bf16[16,4,128,128]{3,2,1,0:T(8,128)(2,1)S(1)} custom-call(bf16[8,128,2048]{2,1,0:T(8,128)(2,1)S(1)} %copy-done.12, bf16[2048,2048]{1,0:T(8,128)(2,1)S(1)} %copy-done.5), custom_call_target="tpu_custom_call" | custom-call | flops 4294967296 | bytes 12582912 | tf_op jit(solution)/shard_map/half_ladder/half_ladder/pallas_call | solution.py:58
  127.1 1.4 copy-done.15
  128.5 13.2 %all-to-all-done.3.h_ref = bf16[16,4,128,128]{3,2,1,0:T(8,128)(2,1)S(1)} async-done(((bf16[16,4,128,128]{3,2,1,0:T(8,128)(2,1)}), bf16[16,4,128,128]{3,2,1,0:T(8,128)(2,1)S(1)}, u32[]{:S(2)}, u32[]{:S(2)}) %all-to-all-start.3) | async-done | bytes 2097184 | tf_op jit(solution)/shard_map/half_ladder/all_to_all | solution.py:235
  141.6 1.3 copy-done.13
  143.0 7.7 %all-to-all-start.2 = ((bf16[16,4,128,128]{3,2,1,0:T(8,128)(2,1)}), bf16[16,4,128,128]{3,2,1,0:T(8,128)(2,1)S(1)}, u32[]{:S(2)}, u32[]{:S(2)}) async-start(bf16[16,4,128,128]{3,2,1,0:T(8,128)(2,1)} %copy-done.15), calls=%async_computation.2 | async-start | bytes 4194304 | tf_op jit(solution)/shard_map/half_ladder/all_to_all | solution.py:235
  151.8 2.2 %copy-done = bf16[16,8,128,128]{3,2,1,0:T(8,128)(2,1)S(1)} copy-done((bf16[16,8,128,128]{3,2,1,0:T(8,128)(2,1)S(1)}, bf16[16,8,128,128]{3,2,1,0:T(8,128)(2,1)}, u32[]{:S(2)}) %copy-start) | copy-done | bytes 4194328
  154.0 3.4 %copy-done.8 = bf16[2048,2048]{1,0:T(8,128)(2,1)S(1)} copy-done((bf16[2048,2048]{1,0:T(8,128)(2,1)S(1)}, bf16[2048,2048]{1,0:T(8,128)(2,1)}, u32[]{:S(2)}) %copy-start.8) | copy-done | bytes 8388632
  157.4 5.8 %cycle_part.1.part_ref = f32[2,2048,256]{2,1,0:T(8,128)S(1)} custom-call(bf16[2048,2048]{1,0:T(8,128)(2,1)S(1)} %copy-done.8, bf16[16,8,128,128]{3,2,1,0:T(8,128)(2,1)S(1)} %copy-done), custom_call_target="tpu_custom_call" | custom-call | flops 4294967296 | bytes 14680064 | tf_op jit(solution)/shard_map/update/cycle_part/pallas_call | solution.py:177
  163.2 2.0 %copy-done.2 = f32[2,2048,256]{2,1,0:T(8,128)} copy-done((f32[2,2048,256]{2,1,0:T(8,128)}, f32[2,2048,256]{2,1,0:T(8,128)S(1)}, u32[]{:S(2)}) %copy-start.2) | copy-done | bytes 4194328
  165.2 3.4 %copy-done.9 = bf16[2048,2048]{1,0:T(8,128)(2,1)S(1)} copy-done((bf16[2048,2048]{1,0:T(8,128)(2,1)S(1)}, bf16[2048,2048]{1,0:T(8,128)(2,1)}, u32[]{:S(2)}) %copy-start.9) | copy-done | bytes 8388632
  168.6 11.5 %update_whole.1.previous_ref = bf16[8,2048,128]{2,1,0:T(8,128)(2,1)} custom-call(f32[8]{0:T(128)S(1)} %copy-done.17, bf16[2048,2048]{1,0:T(8,128)(2,1)S(1)} %copy-done.9, bf16[2048,2048]{1,0:T(8,128)(2,1)S(1)} %copy-done.6, bf16[16,8,128,128]{3,2,1,0:T(8,128)(2,1)S(1)} %copy-done.1, bf16[16,4,128,128]{3,2,1,0:T(8,128)(2,1)S(1)} %copy-done.14, ...), custom_call_target="tpu_custom_call" | custom-call | flops 8589934592 | bytes 23068672 | tf_op jit(solution)/shard_map/update/update_whole/pallas_call | solution.py:160
  180.1 2.2 %copy-done.3 = f32[2,2048,256]{2,1,0:T(8,128)S(1)} copy-done((f32[2,2048,256]{2,1,0:T(8,128)S(1)}, f32[2,2048,256]{2,1,0:T(8,128)}, u32[]{:S(2)}) %copy-start.3) | copy-done | bytes 4194328
  182.3 3.4 %copy-done.7 = bf16[2048,2048]{1,0:T(8,128)(2,1)S(1)} copy-done((bf16[2048,2048]{1,0:T(8,128)(2,1)S(1)}, bf16[2048,2048]{1,0:T(8,128)(2,1)}, u32[]{:S(2)}) %copy-start.7) | copy-done | bytes 8388632
  185.7 7.1 %update_ladder.1 = bf16[8,2048,128]{2,1,0:T(8,128)(2,1)} custom-call(f32[8]{0:T(128)S(1)} %copy-done.17, bf16[2048,2048]{1,0:T(8,128)(2,1)S(1)} %copy-done.7, bf16[16,4,128,128]{3,2,1,0:T(8,128)(2,1)S(1)} %all-to-all-done.2.h_ref, f32[2,2048,256]{2,1,0:T(8,128)S(1)} %copy-done.3, ...), custom_call_target="tpu_custom_call", output_to_operand_aliasing={{}: (6, {})} | custom-call | flops 4294967296 | bytes 14680064 | tf_op jit(solution)/shard_map/update/update_ladder/pallas_call | solution.py:194
  (43 shorter events, 4.7 us)
Async XLA Ops:
  6.5 93.9 %all-gather.3.cloned.1.call-start = ((), (), s32[]{:S(2)}) async-start(), calls=%async_computation.4 | async-start | bytes 9437184 | tf_op jit(solution)/shard_map/gather_ladder/all_gather | solution.py:225
  43.9 107.9 %all-gather.5.cloned.1.call-start = ((), (), s32[]{:S(2)}) async-start(), calls=%async_computation.5 | async-start | bytes 9437184 | tf_op jit(solution)/shard_map/gather_cycle/all_gather | solution.py:231
  43.9 2.2 %copy-start.10 = (bf16[8,128,2048]{2,1,0:T(8,128)(2,1)S(1)}, bf16[8,128,2048]{2,1,0:T(8,128)(2,1)}, u32[]{:S(2)}) copy-start(bf16[8,128,2048]{2,1,0:T(8,128)(2,1)} %a_ref.2) | copy-start | bytes 12582916
  100.4 3.4 %copy-start.4 = (bf16[2048,2048]{1,0:T(8,128)(2,1)S(1)}, bf16[2048,2048]{1,0:T(8,128)(2,1)}, u32[]{:S(2)}) copy-start(bf16[2048,2048]{1,0:T(8,128)(2,1)} %all-gather.3.cloned.1.call-done.l_ref) | copy-start | bytes 25165828
  103.8 2.2 %copy-start.11 = (bf16[8,128,2048]{2,1,0:T(8,128)(2,1)S(1)}, bf16[8,128,2048]{2,1,0:T(8,128)(2,1)}, u32[]{:S(2)}) copy-start(bf16[8,128,2048]{2,1,0:T(8,128)(2,1)} %a_ref.2) | copy-start | bytes 12582916
  111.2 1.3 copy-start.16
  112.5 29.2 %all-to-all-start.3 = ((bf16[16,4,128,128]{3,2,1,0:T(8,128)(2,1)}), bf16[16,4,128,128]{3,2,1,0:T(8,128)(2,1)S(1)}, u32[]{:S(2)}, u32[]{:S(2)}) async-start(bf16[16,4,128,128]{3,2,1,0:T(8,128)(2,1)} %copy-done.16), calls=%async_computation.3 | async-start | bytes 4194304 | tf_op jit(solution)/shard_map/half_ladder/all_to_all | solution.py:235
  116.2 3.5 %copy-start.5 = (bf16[2048,2048]{1,0:T(8,128)(2,1)S(1)}, bf16[2048,2048]{1,0:T(8,128)(2,1)}, u32[]{:S(2)}) copy-start(bf16[2048,2048]{1,0:T(8,128)(2,1)} %all-gather.3.cloned.1.call-done.l_ref) | copy-start | bytes 25165828
  119.7 2.2 %copy-start.12 = (bf16[8,128,2048]{2,1,0:T(8,128)(2,1)S(1)}, bf16[8,128,2048]{2,1,0:T(8,128)(2,1)}, u32[]{:S(2)}) copy-start(bf16[8,128,2048]{2,1,0:T(8,128)(2,1)} %a_ref.2) | copy-start | bytes 12582916
  127.1 1.4 copy-start.15
  128.5 22.2 %copy-start.19 = (s32[8,32,2]{1,2,0:T(2,128)S(1)}, s32[8,32,2]{1,2,0:T(2,128)}, u32[]{:S(2)}) copy-start(s32[8,32,2]{1,2,0:T(2,128)} %param.11) | copy-start | bytes 6148
  128.5 22.9 %copy-start.18 = (f32[2048]{0:T(1024)S(1)}, f32[2048]{0:T(1024)}, u32[]{:S(2)}) copy-start(f32[2048]{0:T(1024)} %param.9) | copy-start | bytes 24580
  141.6 1.3 copy-start.13
  143.0 37.1 %all-to-all-start.2 = ((bf16[16,4,128,128]{3,2,1,0:T(8,128)(2,1)}), bf16[16,4,128,128]{3,2,1,0:T(8,128)(2,1)S(1)}, u32[]{:S(2)}, u32[]{:S(2)}) async-start(bf16[16,4,128,128]{3,2,1,0:T(8,128)(2,1)} %copy-done.15), calls=%async_computation.2 | async-start | bytes 4194304 | tf_op jit(solution)/shard_map/half_ladder/all_to_all | solution.py:235
  151.8 2.2 %copy-start = (bf16[16,8,128,128]{3,2,1,0:T(8,128)(2,1)S(1)}, bf16[16,8,128,128]{3,2,1,0:T(8,128)(2,1)}, u32[]{:S(2)}) copy-start(bf16[16,8,128,128]{3,2,1,0:T(8,128)(2,1)} %all_to_all.21.a_ref) | copy-start | bytes 12582916
  154.0 3.4 %copy-start.8 = (bf16[2048,2048]{1,0:T(8,128)(2,1)S(1)}, bf16[2048,2048]{1,0:T(8,128)(2,1)}, u32[]{:S(2)}) copy-start(bf16[2048,2048]{1,0:T(8,128)(2,1)} %all-gather.5.cloned.1.call-done.k_ref) | copy-start | bytes 25165828
  157.4 7.8 %copy-start.1 = (bf16[16,8,128,128]{3,2,1,0:T(8,128)(2,1)S(1)}, bf16[16,8,128,128]{3,2,1,0:T(8,128)(2,1)}, u32[]{:S(2)}) copy-start(bf16[16,8,128,128]{3,2,1,0:T(8,128)(2,1)} %all_to_all.21.a_ref) | copy-start | bytes 12582916
  157.4 7.8 %copy-start.6 = (bf16[2048,2048]{1,0:T(8,128)(2,1)S(1)}, bf16[2048,2048]{1,0:T(8,128)(2,1)}, u32[]{:S(2)}) copy-start(bf16[2048,2048]{1,0:T(8,128)(2,1)} %all-gather.3.cloned.1.call-done.l_ref) | copy-start | bytes 25165828
  157.4 7.8 %copy-start.14 = (bf16[16,4,128,128]{3,2,1,0:T(8,128)(2,1)S(1)}, bf16[16,4,128,128]{3,2,1,0:T(8,128)(2,1)}, u32[]{:S(2)}) copy-start(bf16[16,4,128,128]{3,2,1,0:T(8,128)(2,1)} %copy-done.13) | copy-start | bytes 6291460
  157.4 7.8 %copy-start.17 = (f32[8]{0:T(128)S(1)}, f32[8]{0:T(128)}, u32[]{:S(2)}) copy-start(f32[8]{0:T(128)} %energy_ref.3) | copy-start | bytes 100
  163.2 2.0 %copy-start.2 = (f32[2,2048,256]{2,1,0:T(8,128)}, f32[2,2048,256]{2,1,0:T(8,128)S(1)}, u32[]{:S(2)}) copy-start(f32[2,2048,256]{2,1,0:T(8,128)S(1)} %cycle_part.1.part_ref) | copy-start | bytes 12582916
  165.2 3.4 %copy-start.9 = (bf16[2048,2048]{1,0:T(8,128)(2,1)S(1)}, bf16[2048,2048]{1,0:T(8,128)(2,1)}, u32[]{:S(2)}) copy-start(bf16[2048,2048]{1,0:T(8,128)(2,1)} %all-gather.5.cloned.1.call-done.k_ref) | copy-start | bytes 25165828
  180.1 2.2 %copy-start.3 = (f32[2,2048,256]{2,1,0:T(8,128)S(1)}, f32[2,2048,256]{2,1,0:T(8,128)}, u32[]{:S(2)}) copy-start(f32[2,2048,256]{2,1,0:T(8,128)} %copy-done.2) | copy-start | bytes 12582916
  182.3 3.4 %copy-start.7 = (bf16[2048,2048]{1,0:T(8,128)(2,1)S(1)}, bf16[2048,2048]{1,0:T(8,128)(2,1)}, u32[]{:S(2)}) copy-start(bf16[2048,2048]{1,0:T(8,128)(2,1)} %all-gather.3.cloned.1.call-done.l_ref) | copy-start | bytes 25165828
Sparse Core Ops, SparseCore 0:
  44.0 50.1 all-gather.2
  100.5 50.5 all-gather.4

commit v2 on v0

v2 whole, which is shorter than its diff:
```python
import functools

import jax
import jax.numpy as jnp
from jax import lax
from jax.experimental import pallas as pl
from jax.experimental.pallas import tpu as pltpu
from jax.sharding import PartitionSpec as P

TILE = 64
LANES = 128
CHUNKS = 2
MIB = 1024 * 1024
SMALL = pl.CostEstimate(flops=1, bytes_accessed=1, transcendentals=0)


def params(mib):
    return pltpu.CompilerParams(vmem_limit_bytes=mib * MIB)


def z_shift(pairs, k):
    return [(p, (p + 2 * k) % pairs) for p in range(pairs)]


def other_core(pairs):
    return [(p, p ^ 1) for p in range(pairs)]


PLACES = [(0, 0), (0, 1), (1, 0), (3, 1), (1, 1), (3, 0), (2, 0), (2, 1)]


def chip_of(pair, back, chips):
    return lax.rem(lax.div(pair, 2) - back + chips, chips)


def owner_of(pair, back, side, chips):
    core = lax.rem(pair, 2)
    return 2 * chip_of(pair, back, chips) + (1 - core if side else core)


def fetch_parts(pair, refs, panel, sems, backs=(0, 1, 2, 3)):
    chips = panel.shape[0] // 2
    for side in range(2):
        for i, (back, half) in enumerate(PLACES):
            if back not in backs:
                continue
            part = refs[side * len(PLACES) + i]
            rows = part.shape[0]
            target = panel.at[owner_of(pair, back, side, chips), pl.ds(half * rows, rows)]
            pltpu.make_async_copy(part, target, sems.at[side * chips + back]).start()


def wait_block(pair, back, side, panel, sems):
    chips = panel.shape[0] // 2
    block = panel.at[owner_of(pair, back, side, chips)]
    pltpu.make_async_copy(block, block, sems.at[side * chips + back]).wait()


def panel_shape(parts):
    rows, columns = parts[0].shape
    return (len(parts) // 2, 2 * rows, columns)


def split_kernel(a_ref, out_ref):
    pairs, rows, _ = a_ref.shape
    for v in range(out_ref.shape[0]):
        out_ref[v] = a_ref[:, :, v * LANES : (v + 1) * LANES].reshape(pairs * rows, LANES)


def split_columns(amplitudes):
    pairs, rows, columns = amplitudes.shape
    whole = pl.BlockSpec(memory_space=pltpu.VMEM)
    return pl.pallas_call(
        split_kernel,
        in_specs=[whole],
        out_specs=whole,
        out_shape=jax.ShapeDtypeStruct((columns // LANES, pairs * rows, LANES), amplitudes.dtype),
        compiler_params=params(8),
        cost_estimate=SMALL,
        name="split_columns",
    )(amplitudes)


def half_kernel(first, place_ref, a_ref, *refs):
    out_ref, left_ref, panel, left_done, sems = refs[-5:]
    ranks = panel.shape[0]
    width = out_ref.shape[0] // ranks
    fetch = pltpu.make_async_copy(a_ref.at[pl.ds(first, left_ref.shape[0])], left_ref, left_done)
    fetch.start()
    fetch_parts(place_ref[0], refs[:-5], panel, sems)
    fetch.wait()
    for side in range(2):
        for back in range(ranks // 2):
            wait_block(place_ref[0], back, side, panel, sems)
    left = left_ref[...].reshape(out_ref.shape[1], left_ref.shape[2])
    for rank in range(ranks):
        result = lax.dot_general(
            left, panel[rank], (((1,), (1,)), ((), ())), preferred_element_type=jnp.float32
        ).astype(jnp.bfloat16)
        for j in range(width):
            out_ref[rank * width + j] = result[:, j * LANES : (j + 1) * LANES]


def half_ladder(amplitudes, own, other, first, count):
    anywhere = pl.BlockSpec(memory_space=pl.ANY)
    _, rows, depth = amplitudes.shape
    parts = [*own, *other]
    shape = (depth // LANES, count * rows, LANES)
    return pl.pallas_call(
        functools.partial(half_kernel, first),
        grid=(1,),
        in_specs=[pl.BlockSpec(memory_space=pltpu.SMEM)] + [anywhere] * (1 + len(parts)),
        out_specs=pl.BlockSpec(shape, lambda i: (0, 0, 0)),
        out_shape=jax.ShapeDtypeStruct(shape, jnp.bfloat16),
        scratch_shapes=[
            pltpu.VMEM((count, rows, depth), jnp.bfloat16),
            pltpu.VMEM(panel_shape(parts), jnp.bfloat16),
            pltpu.SemaphoreType.DMA,
            pltpu.SemaphoreType.DMA((len(own),)),
        ],
        compiler_params=params(60),
        cost_estimate=pl.CostEstimate(
            flops=2 * count * rows * depth * depth, bytes_accessed=depth * depth * 2, transcendentals=0
        ),
        name="half_ladder",
    )(lax.axis_index("pair").reshape(1), amplitudes, *parts)


def widen(source, target):
    owners = source.shape[0]
    rows = target.shape[1] // owners
    for q in range(target.shape[0]):
        for side in range(2):
            r = 2 * q + side
            target[q, :, side * LANES : (side + 1) * LANES] = source[
                :, r * rows : (r + 1) * rows, :
            ].reshape(owners * rows, LANES)


def finish(first, total, q, energy_ref, base_ref, screen_ref, out_ref):
    height = total.shape[0]
    for side in range(2):
        r = 2 * q + side
        screen = jnp.broadcast_to(
            screen_ref[r][:, None, :], (height // TILE, TILE, LANES)
        ).reshape(height, LANES)
        masked = total[:, side * LANES : (side + 1) * LANES] * screen
        out_ref[r] = (masked / (base_ref[...] - energy_ref[first + r])).astype(out_ref.dtype)


BACKS = (0, 1, 3, 2)


def back_of(step):
    return jnp.where(step == 2, 3, jnp.where(step == 3, 2, step))


def main_kernel(place_ref, energy_ref, a_ref, h_ref, base_ref, screen_ref, *refs):
    parts = len(PLACES) * 2
    k_parts, l_parts = refs[:parts], refs[parts : 2 * parts]
    out_ref, next_ref, ladder_ref, k_panel, l_panel, a_wide, h_wide, k_sems, l_sems, store_sems = refs[
        2 * parts :
    ]
    i = pl.program_id(0)
    pair = place_ref[0]
    chips = len(BACKS)

    @pl.when(i == 0)
    def _():
        for back in BACKS:
            fetch_parts(pair, k_parts, k_panel, k_sems, (back,))
            fetch_parts(pair, l_parts, l_panel, l_sems, (back,))
        widen(a_ref, a_wide)
        widen(h_ref, h_wide)

    def store(owner):
        return pltpu.make_async_copy(l_panel.at[owner], ladder_ref.at[owner], store_sems.at[owner])

    back = back_of(i)
    for side in range(2):
        wait_block(pair, back, side, k_panel, k_sems)
        wait_block(pair, back, side, l_panel, l_sems)
        store(owner_of(pair, back, side, chips)).start()
    rows = pl.ds(2 * chip_of(pair, back, chips), 2)
    k = k_panel[rows].reshape(HEIGHT, k_panel.shape[2])
    l = l_panel[rows].reshape(HEIGHT, l_panel.shape[2])
    ready = h_wide.shape[0]
    for q in range(a_wide.shape[0]):
        total = jnp.dot(k, a_wide[q], preferred_element_type=jnp.float32)
        if q < ready:
            total += jnp.dot(l, h_wide[q], preferred_element_type=jnp.float32)
            finish(0, total, q, energy_ref, base_ref, screen_ref, out_ref)
        else:
            next_ref[q - ready] = total

    @pl.when(i == pl.num_programs(0) - 1)
    def _():
        for owner in range(l_panel.shape[0]):
            store(owner).wait()


def ladder_kernel(first, energy_ref, l_ref, h_ref, part_ref, base_ref, screen_ref, previous_ref, out_ref, h_wide):
    del previous_ref

    @pl.when(pl.program_id(0) == 0)
    def _():
        widen(h_ref, h_wide)

    for q in range(h_wide.shape[0]):
        total = part_ref[q] + jnp.dot(l_ref[...], h_wide[q], preferred_element_type=jnp.float32)
        finish(first, total, q, energy_ref, base_ref, screen_ref, out_ref)


HEIGHT = 512


def update_main(pair_energy, cycle_parts, ladder_parts, amps, half, base, screen):
    owners, height, _ = amps.shape
    pairs = pair_energy.shape[0]
    rows = height // pairs
    virt = owners * rows
    count = half.shape[1] // rows
    wide = [pltpu.VMEM((n // 2, virt, 2 * LANES), jnp.bfloat16) for n in (pairs, count)]
    anywhere = pl.BlockSpec(memory_space=pl.ANY)
    panel = panel_shape(cycle_parts)
    chips = len(BACKS)

    def chip(i, place):
        return chip_of(place[0], back_of(i), chips)

    def once(block):
        return pl.BlockSpec(block.shape, lambda i, place: (0, 0, 0), pipeline_mode=pl.Buffered(1))

    grid_spec = pltpu.PrefetchScalarGridSpec(
        num_scalar_prefetch=1,
        grid=(chips,),
        in_specs=[
            pl.BlockSpec(memory_space=pltpu.SMEM),
            once(amps),
            once(half),
            pl.BlockSpec((HEIGHT, LANES), lambda i, place: (chip(i, place), 0)),
            pl.BlockSpec((count, HEIGHT // TILE, LANES), lambda i, place: (0, chip(i, place), 0)),
        ]
        + [anywhere] * (len(cycle_parts) + len(ladder_parts)),
        out_specs=[
            pl.BlockSpec((count, HEIGHT, LANES), lambda i, place: (0, chip(i, place), 0)),
            pl.BlockSpec(
                ((pairs - count) // 2, HEIGHT, 2 * LANES), lambda i, place: (0, chip(i, place), 0)
            ),
            anywhere,
        ],
        scratch_shapes=[
            pltpu.VMEM(panel, jnp.bfloat16),
            pltpu.VMEM(panel, jnp.bfloat16),
            *wide,
        ]
        + [pltpu.SemaphoreType.DMA((panel[0],))] * 3,
    )
    return pl.pallas_call(
        main_kernel,
        grid_spec=grid_spec,
        out_shape=[
            jax.ShapeDtypeStruct((pairs, virt, LANES), jnp.bfloat16),
            jax.ShapeDtypeStruct(((pairs - count) // 2, virt, 2 * LANES), jnp.float32),
            jax.ShapeDtypeStruct(panel, jnp.bfloat16),
        ],
        compiler_params=params(60),
        cost_estimate=SMALL,
        name="update_main",
    )(
        lax.axis_index("pair").reshape(1), pair_energy, amps, half, base, screen,
        *cycle_parts, *ladder_parts,
    )


def update_ladder(pair_energy, ladder, half, part, base, screen, previous, first):
    owners = half.shape[0]
    virt = ladder.shape[0]
    count = half.shape[1] // (virt // owners)
    group = first // count
    height = HEIGHT
    return pl.pallas_call(
        functools.partial(ladder_kernel, first),
        grid=(virt // height,),
        in_specs=[
            pl.BlockSpec(memory_space=pltpu.SMEM),
            pl.BlockSpec((height, virt), lambda i: (i, 0)),
            pl.BlockSpec(half.shape, lambda i: (0, 0, 0)),
            pl.BlockSpec((count // 2, height, 2 * LANES), lambda i: (0, i, 0)),
            pl.BlockSpec((height, LANES), lambda i: (i, 0)),
            pl.BlockSpec((count, height // TILE, LANES), lambda i: (group, i, 0)),
            pl.BlockSpec(memory_space=pl.ANY),
        ],
        out_specs=pl.BlockSpec((count, height, LANES), lambda i: (group, i, 0)),
        out_shape=jax.ShapeDtypeStruct(previous.shape, previous.dtype),
        scratch_shapes=[pltpu.VMEM((count // 2, virt, 2 * LANES), jnp.bfloat16)],
        input_output_aliases={6: 0},
        compiler_params=params(60),
        cost_estimate=SMALL,
        name="update_ladder",
    )(pair_energy, ladder, half, part, base, screen, previous)


def local(amplitudes, cycle_panel, ladder_panel, virt_energy, pair_energy, tile_mask):
    pairs = amplitudes.shape[0]
    count = pairs // CHUNKS
    exchange = functools.partial(
        lax.all_to_all, axis_name="virt", split_axis=0, concat_axis=0, tiled=True
    )
    after = lax.optimization_barrier
    v = lax.axis_index("virt")
    rows, columns = ladder_panel.shape
    owners = columns // LANES
    ranks = virt_energy.shape[0] // (owners * rows)

    def along(part, step):
        return lax.ppermute(part, "pair", z_shift(ranks, step))

    def across(parts):
        return [lax.ppermute(part, "pair", other_core(ranks)) for part in parts]

    def first_parts(top, bottom):
        return [along(top, 1), along(bottom, 3)]

    def last_parts(top, bottom, first):
        return [along(bottom, 1), along(top, 3), along(first[0], 1), along(first[1], 3)]

    with jax.named_scope("spread_panels"):
        both = jnp.concatenate([ladder_panel, cycle_panel])
        both = exchange(jnp.broadcast_to(both[None], (owners, 2 * rows, columns)))
        middle = owners // 2
        halves = [
            both[i * middle : (i + 1) * middle, j * rows : (j + 1) * rows].reshape(-1, columns)
            for j in range(2)
            for i in range(2)
        ]
        halves, own = after((halves, amplitudes))
        ladder_halves, cycle_halves = halves[:2], halves[2:]
    with jax.named_scope("exchange_amplitudes"):
        amps = exchange(split_columns(own))
    with jax.named_scope("update"):
        virt_energy, tile_mask, _ = after((virt_energy, tile_mask, halves))
        column_energy = lax.dynamic_slice_in_dim(virt_energy, v * LANES, LANES)
        base = virt_energy[:, None] + column_energy[None, :]
        screen = jnp.repeat(tile_mask.astype(jnp.float32), TILE, axis=2)
    with jax.named_scope("gather_ladder"):
        first = first_parts(*ladder_halves)
        other = across(ladder_halves)
        first, other = after((first, other))
        last = last_parts(*ladder_halves, first)
        other += across(first)
        last, cycle_halves = after((last, cycle_halves))
        mine, other = ladder_halves + first + last, other + across(last)
    with jax.named_scope("gather_cycle"):
        first = first_parts(*cycle_halves)
    with jax.named_scope("half_ladder"):
        sent = half_ladder(amplitudes, mine, other, 0, count)
        sent, first, own, amps, base, screen = after((sent, first, amplitudes, amps, base, screen))
        half = exchange(sent)
    with jax.named_scope("gather_cycle"):
        last = last_parts(*cycle_halves, first)
        close = across(cycle_halves + first)
    with jax.named_scope("half_ladder"):
        sent = half_ladder(own, mine, other, count, count)
        last, sent = after((last, sent))
        half_tail = exchange(sent)
    with jax.named_scope("gather_cycle"):
        cycle_parts = cycle_halves + first + last + close + across(last)
    with jax.named_scope("update"):
        out, part, ladder = update_main(
            pair_energy, cycle_parts, mine + other, amps, half, base, screen
        )
        ladder = ladder.reshape(-1, columns)
        return update_ladder(pair_energy, ladder, half_tail, part, base, screen, out, count)


def solution(mesh):
    in_specs = (
        P("pair", "virt", None),
        P(("pair", "virt"), None),
        P(("pair", "virt"), None),
        P(),
        P("pair"),
        P("pair", None, "virt"),
    )
    out_specs = P("pair", None, "virt")
    return jax.shard_map(local, mesh=mesh, in_specs=in_specs, out_specs=out_specs, check_vma=False)
```

time: 275 us -> 186 us (0.68)
  waiting for transfers between devices: 130 us -> 47.7 us
  local copies, waits for them, and re-layouts: 71.4 us -> 5.99 us
  Pallas kernels: 0 us -> 51.3 us
  matrix products: 46.6 us -> 0 us
  blocking collectives: 0 us -> 35 us
  starting transfers between devices: 12.4 us -> 43.1 us
  between operations: 13.5 us -> 0.28 us
    all_gather x2 -> x0, waiting for transfers between devices: 100 us -> none  [the longest x1 100 us: local(): lax.all_gather(ladder_panel, ('pair', 'virt'), axis=0, tiled=True)]
    pallas_call x0 -> x5, Pallas kernels: none -> 51.3 us  [the longest x1 20.6 us: update_main(): pl.pallas_call(main_kernel, grid_spec=grid_spec, out_shape=[jax.ShapeDtyp...]
    dot_general x3 -> x0, matrix products: 46.6 us -> none  [the longest x1 18.1 us: local(): jnp.einsum('ac,rcb->rab', full_cycle, amps_virt, preferred_element_type=j...]
    ppermute x0 -> x28, waiting for transfers between devices: none -> 42.4 us  [the longest x12 37.9 us: along(): return lax.ppermute(part, 'pair', z_shift(ranks, step))]
    all_to_all x0 -> x1, blocking collectives: none -> 35 us  [local(): both = exchange(jnp.broadcast_to(both[None], (owners, 2 * rows, columns)))]
    all_to_all x4 -> x0, local copies, waits for them, and re-layouts: 28.5 us -> none  [the longest x2 14.3 us: local(): lax.all_to_all(half_ladder, 'virt', split_axis=2, concat_axis=1, tiled=True)]
    ppermute x0 -> x28, starting transfers between devices: none -> 27.5 us  [the longest x12 16.8 us: along(): return lax.ppermute(part, 'pair', z_shift(ranks, step))]
    all_to_all x2 -> x3, waiting for transfers between devices: 28.3 us -> 5.33 us  [the longest x1 5.07 us: local(): half = exchange(sent)]
  transfers between devices with their start and end apart: 4 -> 31, of which waited for: 2 -> 12; matrix products, arithmetic and copies ran while one was open for 29% -> 1% of each run, Pallas kernels for 0% -> 22%
where the time goes in v2:
time: 186 us
  Pallas kernels  51.3 us (28%)
  waiting for transfers between devices  47.7 us (26%)
  starting transfers between devices  43.1 us (23%)
  blocking collectives  35 us (19%)
  local copies, waits for them, and re-layouts  5.99 us (3%)
  other arithmetic  2.19 us (1%)
    ppermute x12, waiting for transfers between devices, along(): return lax.ppermute(part, 'pair', z_shift(ranks, step))  37.9 us
    all_to_all x1, blocking collectives, local(): both = exchange(jnp.broadcast_to(both[None], (owners, 2 * rows, columns)))  35 us
    pallas_call x1, Pallas kernels, update_main(): pl.pallas_call(main_kernel, grid_spec=grid_spec, out_shape=[jax.ShapeDtyp...  20.6 us
    pallas_call x2, Pallas kernels, half_ladder(): pl.pallas_call(functools.partial(half_kernel, first), grid=(1,), in_specs...  19.8 us
    ppermute x12, starting transfers between devices, along(): return lax.ppermute(part, 'pair', z_shift(ranks, step))  16.8 us
    ppermute x16, starting transfers between devices, across(): return [lax.ppermute(part, 'pair', other_core(ranks)) for part in parts]  10.7 us
    pallas_call x1, Pallas kernels, update_ladder(): pl.pallas_call(functools.partial(ladder_kernel, first), grid=(virt // hei...  10 us
    all_to_all x1, starting transfers between devices, local(): half = exchange(sent)  6.49 us
  transfers between devices with their start and end apart: 31, of which 12 were waited for; matrix products, arithmetic and copies ran while one was open for 1% of the time, Pallas kernels for 22%

profile of v2, /device:TPU:1, one launch (start us, length us, event | category | flops | bytes accessed | tf_op | source)
XLA Modules:
  0.0 185.5 jit_solution(10220347880092188090)
XLA Ops:
  1.1 35.0 %all_to_all.20 = bf16[16,32,2048]{2,1,0:T(8,128)(2,1)S(1)} all-to-all(bf16[16,32,2048]{2,1,0:T(8,128)(2,1)S(1)} %broadcast_in_dim.4), channel_id=1, replica_groups=mesh['pair'=8,'virt'=16] {'virt'}, dimensions={0} | all-to-all | bytes 4194304 | tf_op jit(solution)/shard_map/spread_panels/all_to_all | solution.py:330
  37.3 2.0 %copy-done = bf16[16,1024,128]{2,1,0:T(8,128)(2,1)} copy-done((bf16[16,1024,128]{2,1,0:T(8,128)(2,1)}, bf16[16,1024,128]{2,1,0:T(8,128)(2,1)S(1)}, u32[]{:S(2)}) %copy-start) | copy-done | bytes 4194328
  39.3 4.7 %all-to-all-start.1 = ((bf16[16,1024,128]{2,1,0:T(8,128)(2,1)}), bf16[16,1024,128]{2,1,0:T(8,128)(2,1)}, u32[]{:S(2)}, u32[]{:S(2)}) async-start(bf16[16,1024,128]{2,1,0:T(8,128)(2,1)} %copy-done), calls=%async_computation.1 | async-start | bytes 8388608 | tf_op jit(solution)/shard_map/exchange_amplitudes/all_to_all | solution.py:340
  44.0 2.1 %collective-permute-start.2 = (bf16[128,2048]{1,0:T(8,128)(2,1)S(1)}, bf16[128,2048]{1,0:T(8,128)(2,1)S(1)}, u32[]{:S(2)}, u32[]{:S(2)}) collective-permute-start(bf16[128,2048]{1,0:T(8,128)(2,1)S(1)} %bitcast.21), channel_id=1, source_target_pairs={{0,16},{16,0},{32,48},{48,32},{64,80},{80,64},{96,112},{112,96},{1... | collective-permute-start | bytes 1572872 | tf_op jit(solution)/shard_map/gather_ladder/ppermute | solution.py:320
  46.1 1.7 collective-permute-start
  48.1 1.9 %collective-permute-start.1 = (bf16[128,2048]{1,0:T(8,128)(2,1)S(1)}, bf16[128,2048]{1,0:T(8,128)(2,1)}, u32[]{:S(2)}, u32[]{:S(2)}) collective-permute-start(bf16[128,2048]{1,0:T(8,128)(2,1)S(1)} %bitcast.16), channel_id=1, source_target_pairs={{0,96},{16,112},{32,0},{48,16},{64,32},{80,48},{96,64},{112,80},{1... | collective-permute-start | bytes 1572872 | tf_op jit(solution)/shard_map/gather_ladder/ppermute | solution.py:317
  50.0 1.7 collective-permute-start.5
  51.7 10.4 %collective-permute-done.refs_2_.refs_18_ = bf16[128,2048]{1,0:T(8,128)(2,1)S(1)} collective-permute-done((bf16[128,2048]{1,0:T(8,128)(2,1)S(1)}, bf16[128,2048]{1,0:T(8,128)(2,1)S(1)}, u32[]{:S(2)}, u32[]{:S(2)}) %collective-permute-start) | collective-permute-done | bytes 524320 | tf_op jit(solution)/shard_map/gather_ladder/ppermute | solution.py:317
  63.2 1.7 collective-permute-start.7
  64.9 1.8 collective-permute-start.8
  66.7 6.5 %collective-permute-done.5.refs_5_.refs_21_ = bf16[128,2048]{1,0:T(8,128)(2,1)} collective-permute-done((bf16[128,2048]{1,0:T(8,128)(2,1)S(1)}, bf16[128,2048]{1,0:T(8,128)(2,1)}, u32[]{:S(2)}, u32[]{:S(2)}) %collective-permute-start.5) | collective-permute-done | bytes 524320 | tf_op jit(solution)/shard_map/gather_ladder/ppermute | solution.py:317
  74.3 10.3 %collective-permute-done.6.refs_6_.refs_22_ = bf16[128,2048]{1,0:T(8,128)(2,1)} collective-permute-done((bf16[128,2048]{1,0:T(8,128)(2,1)S(1)}, bf16[128,2048]{1,0:T(8,128)(2,1)}, u32[]{:S(2)}, u32[]{:S(2)}) %collective-permute-start.6) | collective-permute-done | bytes 524320 | tf_op jit(solution)/shard_map/gather_ladder/ppermute | solution.py:317
  88.0 2.6 %collective-permute-start.15 = (bf16[128,2048]{1,0:T(8,128)(2,1)S(1)}, bf16[128,2048]{1,0:T(8,128)(2,1)}, u32[]{:S(2)}, u32[]{:S(2)}) collective-permute-start(bf16[128,2048]{1,0:T(8,128)(2,1)S(1)} %bitcast.7), channel_id=1, source_target_pairs={{0,96},{16,112},{32,0},{48,16},{64,32},{80,48},{96,64},{112,80},{1... | collective-permute-start | bytes 1572872 | tf_op jit(solution)/shard_map/gather_cycle/ppermute | solution.py:317
  93.3 9.9 %half_ladder.2 = bf16[16,512,128]{2,1,0:T(8,128)(2,1)} custom-call(s32[1]{0:T(128)} %bitcast.place_ref, bf16[8,128,2048]{2,1,0:T(8,128)(2,1)} %a_ref.3, bf16[128,2048]{1,0:T(8,128)(2,1)} %bitcast.24, bf16[128,2048]{1,0:T(8,128)(2,1)} %bitcast.18, bf16[128,2048]{1,0:T(8,128)(2,1)} %copy-done.8, bf16[128,2048]{1,0:T(8,128)(2,1)} %collective-permute-done.1.refs_3_.refs_19_, ...), custom_call_target="tpu_custom_call" | custom-call | flops 4294967296 | bytes 8388608 | tf_op jit(solution)/shard_map/half_ladder/half_ladder/pallas_call | solution.py:109
  103.4 6.5 %all-to-all-start.2 = ((bf16[16,512,128]{2,1,0:T(8,128)(2,1)}), bf16[16,512,128]{2,1,0:T(8,128)(2,1)S(1)}, u32[]{:S(2)}, u32[]{:S(2)}) async-start(bf16[16,512,128]{2,1,0:T(8,128)(2,1)} %half_ladder.2), calls=%async_computation.2 | async-start | bytes 4194304 | tf_op jit(solution)/shard_map/half_ladder/all_to_all | solution.py:359
  109.9 2.1 %collective-permute-start.17 = (bf16[128,2048]{1,0:T(8,128)(2,1)S(1)}, bf16[128,2048]{1,0:T(8,128)(2,1)S(1)}, u32[]{:S(2)}, u32[]{:S(2)}) collective-permute-start(bf16[128,2048]{1,0:T(8,128)(2,1)S(1)} %bitcast.12), channel_id=1, source_target_pairs={{0,96},{16,112},{32,0},{48,16},{64,32},{80,48},{96,64},{112,80},{1... | collective-permute-start | bytes 1572872 | tf_op jit(solution)/shard_map/gather_cycle/ppermute | solution.py:317
  112.0 2.7 %collective-permute-start.19 = (bf16[128,2048]{1,0:T(8,128)(2,1)}, bf16[128,2048]{1,0:T(8,128)(2,1)}, u32[]{:S(2)}, u32[]{:S(2)}) collective-permute-start(bf16[128,2048]{1,0:T(8,128)(2,1)} %collective-permute-done.15.refs_3_), channel_id=1, source_target_pairs={{0,96},{16,112},{32,0},{48,16},{64,32},{80,48},{96,64},{112,80},{1... | collective-permute-start | bytes 1572872 | tf_op jit(solution)/shard_map/gather_cycle/ppermute | solution.py:317
  114.7 9.9 %half_ladder.3 = bf16[16,512,128]{2,1,0:T(8,128)(2,1)} custom-call(s32[1]{0:T(128)} %bitcast.place_ref, bf16[8,128,2048]{2,1,0:T(8,128)(2,1)} %a_ref.3, bf16[128,2048]{1,0:T(8,128)(2,1)} %bitcast.25, bf16[128,2048]{1,0:T(8,128)(2,1)} %bitcast.19, bf16[128,2048]{1,0:T(8,128)(2,1)} %copy-done.8, bf16[128,2048]{1,0:T(8,128)(2,1)} %collective-permute-done.1.refs_3_.refs_19_, ...), custom_call_target="tpu_custom_call" | custom-call | flops 4294967296 | bytes 8388608 | tf_op jit(solution)/shard_map/half_ladder/half_ladder/pallas_call | solution.py:109
  124.7 10.7 %collective-permute-done.18.refs_6_ = bf16[128,2048]{1,0:T(8,128)(2,1)} collective-permute-done((bf16[128,2048]{1,0:T(8,128)(2,1)}, bf16[128,2048]{1,0:T(8,128)(2,1)}, u32[]{:S(2)}, u32[]{:S(2)}) %collective-permute-start.18) | collective-permute-done | bytes 524320 | tf_op jit(solution)/shard_map/gather_cycle/ppermute | solution.py:317
  135.4 5.1 %all-to-all-done.2.h_ref = bf16[16,512,128]{2,1,0:T(8,128)(2,1)S(1)} async-done(((bf16[16,512,128]{2,1,0:T(8,128)(2,1)}), bf16[16,512,128]{2,1,0:T(8,128)(2,1)S(1)}, u32[]{:S(2)}, u32[]{:S(2)}) %all-to-all-start.2) | async-done | bytes 2097184 | tf_op jit(solution)/shard_map/half_ladder/all_to_all | solution.py:359
  140.5 4.4 %all-to-all-start.3 = ((bf16[16,512,128]{2,1,0:T(8,128)(2,1)}), bf16[16,512,128]{2,1,0:T(8,128)(2,1)}, u32[]{:S(2)}, u32[]{:S(2)}) async-start(bf16[16,512,128]{2,1,0:T(8,128)(2,1)} %half_ladder.3), calls=%async_computation.3 | async-start | bytes 4194304 | tf_op jit(solution)/shard_map/half_ladder/all_to_all | solution.py:366
  144.9 2.2 %collective-permute-start.20 = (bf16[128,2048]{1,0:T(8,128)(2,1)S(1)}, bf16[128,2048]{1,0:T(8,128)(2,1)S(1)}, u32[]{:S(2)}, u32[]{:S(2)}) collective-permute-start(bf16[128,2048]{1,0:T(8,128)(2,1)S(1)} %bitcast.13), channel_id=1, source_target_pairs={{0,16},{16,0},{32,48},{48,32},{64,80},{80,64},{96,112},{112,96},{1... | collective-permute-start | bytes 1572872 | tf_op jit(solution)/shard_map/gather_cycle/ppermute | solution.py:320
  154.9 20.6 %update_main.1 = (bf16[8,2048,128]{2,1,0:T(8,128)(2,1)}, f32[2,2048,256]{2,1,0:T(8,128)}, bf16[8,256,2048]{2,1,0:T(8,128)(2,1)}) custom-call(s32[1]{0:T(128)} %bitcast.place_ref, f32[8]{0:T(128)} %energy_ref.3, bf16[16,1024,128]{2,1,0:T(8,128)(2,1)} %all-to-all-done.1.a_ref, bf16[16,512,128]{2,1,0:T(8,128)(2,1)} %copy-done.2, ...), custom_call_target="tpu_custom_call" | custom-call | flops 1 | bytes 1 | tf_op jit(solution)/shard_map/update/update_main/pallas_call | solution.py:259
  175.5 10.0 %update_ladder.1 = bf16[8,2048,128]{2,1,0:T(8,128)(2,1)} custom-call(f32[8]{0:T(128)} %energy_ref.3, bf16[2048,2048]{1,0:T(8,128)(2,1)} %bitcast.6, bf16[16,512,128]{2,1,0:T(8,128)(2,1)} %all-to-all-done.3.h_ref, f32[2,2048,256]{2,1,0:T(8,128)} %get-tuple-element.67.part_ref, ...), custom_call_target="tpu_custom_call", output_to_operand_aliasing={{}: (6, {})} | custom-call | flops 1 | bytes 1 | tf_op jit(solution)/shard_map/update/update_ladder/pallas_call | solution.py:282
  (93 shorter events, 18.9 us)
Async XLA Ops:
  39.3 64.1 %all-to-all-start.1 = ((bf16[16,1024,128]{2,1,0:T(8,128)(2,1)}), bf16[16,1024,128]{2,1,0:T(8,128)(2,1)}, u32[]{:S(2)}, u32[]{:S(2)}) async-start(bf16[16,1024,128]{2,1,0:T(8,128)(2,1)} %copy-done), calls=%async_computation.1 | async-start | bytes 8388608 | tf_op jit(solution)/shard_map/exchange_amplitudes/all_to_all | solution.py:340
  44.0 7.7 %collective-permute-start.2 = (bf16[128,2048]{1,0:T(8,128)(2,1)S(1)}, bf16[128,2048]{1,0:T(8,128)(2,1)S(1)}, u32[]{:S(2)}, u32[]{:S(2)}) collective-permute-start(bf16[128,2048]{1,0:T(8,128)(2,1)S(1)} %bitcast.21), channel_id=1, source_target_pairs={{0,16},{16,0},{32,48},{48,32},{64,80},{80,64},{96,112},{112,96},{1... | collective-permute-start | bytes 1572872 | tf_op jit(solution)/shard_map/gather_ladder/ppermute | solution.py:320
  46.1 16.1 %collective-permute-start = (bf16[128,2048]{1,0:T(8,128)(2,1)S(1)}, bf16[128,2048]{1,0:T(8,128)(2,1)S(1)}, u32[]{:S(2)}, u32[]{:S(2)}) collective-permute-start(bf16[128,2048]{1,0:T(8,128)(2,1)S(1)} %bitcast.22), channel_id=1, source_target_pairs={{0,32},{16,48},{32,64},{48,80},{64,96},{80,112},{96,0},{112,16},{1... | collective-permute-start | bytes 1572872 | tf_op jit(solution)/shard_map/gather_ladder/ppermute | solution.py:317
  47.7 14.4 %collective-permute-start.3 = (bf16[128,2048]{1,0:T(8,128)(2,1)S(1)}, bf16[128,2048]{1,0:T(8,128)(2,1)S(1)}, u32[]{:S(2)}, u32[]{:S(2)}) collective-permute-start(bf16[128,2048]{1,0:T(8,128)(2,1)S(1)} %bitcast.15), channel_id=1, source_target_pairs={{0,16},{16,0},{32,48},{48,32},{64,80},{80,64},{96,112},{112,96},{1... | collective-permute-start | bytes 1572872 | tf_op jit(solution)/shard_map/gather_ladder/ppermute | solution.py:320
  48.1 14.1 %collective-permute-start.1 = (bf16[128,2048]{1,0:T(8,128)(2,1)S(1)}, bf16[128,2048]{1,0:T(8,128)(2,1)}, u32[]{:S(2)}, u32[]{:S(2)}) collective-permute-start(bf16[128,2048]{1,0:T(8,128)(2,1)S(1)} %bitcast.16), channel_id=1, source_target_pairs={{0,96},{16,112},{32,0},{48,16},{64,32},{80,48},{96,64},{112,80},{1... | collective-permute-start | bytes 1572872 | tf_op jit(solution)/shard_map/gather_ladder/ppermute | solution.py:317
  50.0 23.2 %collective-permute-start.5 = (bf16[128,2048]{1,0:T(8,128)(2,1)S(1)}, bf16[128,2048]{1,0:T(8,128)(2,1)}, u32[]{:S(2)}, u32[]{:S(2)}) collective-permute-start(bf16[128,2048]{1,0:T(8,128)(2,1)S(1)} %bitcast.23), channel_id=1, source_target_pairs={{0,96},{16,112},{32,0},{48,16},{64,32},{80,48},{96,64},{112,80},{1... | collective-permute-start | bytes 1572872 | tf_op jit(solution)/shard_map/gather_ladder/ppermute | solution.py:317
  51.7 22.6 %collective-permute-start.4 = (bf16[128,2048]{1,0:T(8,128)(2,1)S(1)}, bf16[128,2048]{1,0:T(8,128)(2,1)}, u32[]{:S(2)}, u32[]{:S(2)}) collective-permute-start(bf16[128,2048]{1,0:T(8,128)(2,1)S(1)} %bitcast.17), channel_id=1, source_target_pairs={{0,32},{16,48},{32,64},{48,80},{64,96},{80,112},{96,0},{112,16},{1... | collective-permute-start | bytes 1572872 | tf_op jit(solution)/shard_map/gather_ladder/ppermute | solution.py:317
  62.2 22.5 %collective-permute-start.6 = (bf16[128,2048]{1,0:T(8,128)(2,1)S(1)}, bf16[128,2048]{1,0:T(8,128)(2,1)}, u32[]{:S(2)}, u32[]{:S(2)}) collective-permute-start(bf16[128,2048]{1,0:T(8,128)(2,1)S(1)} %collective-permute-done.refs_2_.refs_18_), channel_id=1, source_target_pairs={{0,32},{16,48},{32,64},{48,80},{64,96},{80,112},{96,0},{112,16},{1... | collective-permute-start | bytes 1572872 | tf_op jit(solution)/shard_map/gather_ladder/ppermute | solution.py:317
  63.2 21.4 %collective-permute-start.7 = (bf16[128,2048]{1,0:T(8,128)(2,1)}, bf16[128,2048]{1,0:T(8,128)(2,1)}, u32[]{:S(2)}, u32[]{:S(2)}) collective-permute-start(bf16[128,2048]{1,0:T(8,128)(2,1)} %collective-permute-done.1.refs_3_.refs_19_), channel_id=1, source_target_pairs={{0,96},{16,112},{32,0},{48,16},{64,32},{80,48},{96,64},{112,80},{1... | collective-permute-start | bytes 1572872 | tf_op jit(solution)/shard_map/gather_ladder/ppermute | solution.py:317
  64.9 20.9 %collective-permute-start.8 = (bf16[128,2048]{1,0:T(8,128)(2,1)S(1)}, bf16[128,2048]{1,0:T(8,128)(2,1)S(1)}, u32[]{:S(2)}, u32[]{:S(2)}) collective-permute-start(bf16[128,2048]{1,0:T(8,128)(2,1)S(1)} %collective-permute-done.refs_2_.refs_18_), channel_id=1, source_target_pairs={{0,16},{16,0},{32,48},{48,32},{64,80},{80,64},{96,112},{112,96},{1... | collective-permute-start | bytes 1572872 | tf_op jit(solution)/shard_map/gather_ladder/ppermute | solution.py:320
  73.2 13.5 %collective-permute-start.9 = (bf16[128,2048]{1,0:T(8,128)(2,1)}, bf16[128,2048]{1,0:T(8,128)(2,1)S(1)}, u32[]{:S(2)}, u32[]{:S(2)}) collective-permute-start(bf16[128,2048]{1,0:T(8,128)(2,1)} %collective-permute-done.1.refs_3_.refs_19_), channel_id=1, source_target_pairs={{0,16},{16,0},{32,48},{48,32},{64,80},{80,64},{96,112},{112,96},{1... | collective-permute-start | bytes 1572872 | tf_op jit(solution)/shard_map/gather_ladder/ppermute | solution.py:320
  85.3 7.9 %collective-permute-start.11 = (bf16[128,2048]{1,0:T(8,128)(2,1)}, bf16[128,2048]{1,0:T(8,128)(2,1)}, u32[]{:S(2)}, u32[]{:S(2)}) collective-permute-start(bf16[128,2048]{1,0:T(8,128)(2,1)} %collective-permute-done.5.refs_5_.refs_21_), channel_id=1, source_target_pairs={{0,16},{16,0},{32,48},{48,32},{64,80},{80,64},{96,112},{112,96},{1... | collective-permute-start | bytes 1572872 | tf_op jit(solution)/shard_map/gather_ladder/ppermute | solution.py:320
  85.3 7.9 %collective-permute-start.12 = (bf16[128,2048]{1,0:T(8,128)(2,1)}, bf16[128,2048]{1,0:T(8,128)(2,1)}, u32[]{:S(2)}, u32[]{:S(2)}) collective-permute-start(bf16[128,2048]{1,0:T(8,128)(2,1)} %collective-permute-done.6.refs_6_.refs_22_), channel_id=1, source_target_pairs={{0,16},{16,0},{32,48},{48,32},{64,80},{80,64},{96,112},{112,96},{1... | collective-permute-start | bytes 1572872 | tf_op jit(solution)/shard_map/gather_ladder/ppermute | solution.py:320
  85.8 7.4 %collective-permute-start.13 = (bf16[128,2048]{1,0:T(8,128)(2,1)}, bf16[128,2048]{1,0:T(8,128)(2,1)}, u32[]{:S(2)}, u32[]{:S(2)}) collective-permute-start(bf16[128,2048]{1,0:T(8,128)(2,1)} %collective-permute-done.7.refs_7_.refs_23_), channel_id=1, source_target_pairs={{0,16},{16,0},{32,48},{48,32},{64,80},{80,64},{96,112},{112,96},{1... | collective-permute-start | bytes 1572872 | tf_op jit(solution)/shard_map/gather_ladder/ppermute | solution.py:320
  86.7 16.5 %collective-permute-start.14 = (bf16[128,2048]{1,0:T(8,128)(2,1)S(1)}, bf16[128,2048]{1,0:T(8,128)(2,1)}, u32[]{:S(2)}, u32[]{:S(2)}) collective-permute-start(bf16[128,2048]{1,0:T(8,128)(2,1)S(1)} %bitcast.11), channel_id=1, source_target_pairs={{0,32},{16,48},{32,64},{48,80},{64,96},{80,112},{96,0},{112,16},{1... | collective-permute-start | bytes 1572872 | tf_op jit(solution)/shard_map/gather_cycle/ppermute | solution.py:317
  88.0 15.1 %collective-permute-start.15 = (bf16[128,2048]{1,0:T(8,128)(2,1)S(1)}, bf16[128,2048]{1,0:T(8,128)(2,1)}, u32[]{:S(2)}, u32[]{:S(2)}) collective-permute-start(bf16[128,2048]{1,0:T(8,128)(2,1)S(1)} %bitcast.7), channel_id=1, source_target_pairs={{0,96},{16,112},{32,0},{48,16},{64,32},{80,48},{96,64},{112,80},{1... | collective-permute-start | bytes 1572872 | tf_op jit(solution)/shard_map/gather_cycle/ppermute | solution.py:317
  103.4 37.0 %all-to-all-start.2 = ((bf16[16,512,128]{2,1,0:T(8,128)(2,1)}), bf16[16,512,128]{2,1,0:T(8,128)(2,1)S(1)}, u32[]{:S(2)}, u32[]{:S(2)}) async-start(bf16[16,512,128]{2,1,0:T(8,128)(2,1)} %half_ladder.2), calls=%async_computation.2 | async-start | bytes 4194304 | tf_op jit(solution)/shard_map/half_ladder/all_to_all | solution.py:359
  109.9 14.7 %collective-permute-start.17 = (bf16[128,2048]{1,0:T(8,128)(2,1)S(1)}, bf16[128,2048]{1,0:T(8,128)(2,1)S(1)}, u32[]{:S(2)}, u32[]{:S(2)}) collective-permute-start(bf16[128,2048]{1,0:T(8,128)(2,1)S(1)} %bitcast.12), channel_id=1, source_target_pairs={{0,96},{16,112},{32,0},{48,16},{64,32},{80,48},{96,64},{112,80},{1... | collective-permute-start | bytes 1572872 | tf_op jit(solution)/shard_map/gather_cycle/ppermute | solution.py:317
  112.0 12.6 %collective-permute-start.16 = (bf16[128,2048]{1,0:T(8,128)(2,1)S(1)}, bf16[128,2048]{1,0:T(8,128)(2,1)}, u32[]{:S(2)}, u32[]{:S(2)}) collective-permute-start(bf16[128,2048]{1,0:T(8,128)(2,1)S(1)} %bitcast.8), channel_id=1, source_target_pairs={{0,32},{16,48},{32,64},{48,80},{64,96},{80,112},{96,0},{112,16},{1... | collective-permute-start | bytes 1572872 | tf_op jit(solution)/shard_map/gather_cycle/ppermute | solution.py:317
  112.0 23.4 %collective-permute-start.18 = (bf16[128,2048]{1,0:T(8,128)(2,1)}, bf16[128,2048]{1,0:T(8,128)(2,1)}, u32[]{:S(2)}, u32[]{:S(2)}) collective-permute-start(bf16[128,2048]{1,0:T(8,128)(2,1)} %collective-permute-done.14.refs_2_), channel_id=1, source_target_pairs={{0,32},{16,48},{32,64},{48,80},{64,96},{80,112},{96,0},{112,16},{1... | collective-permute-start | bytes 1572872 | tf_op jit(solution)/shard_map/gather_cycle/ppermute | solution.py:317
  112.0 23.4 %collective-permute-start.19 = (bf16[128,2048]{1,0:T(8,128)(2,1)}, bf16[128,2048]{1,0:T(8,128)(2,1)}, u32[]{:S(2)}, u32[]{:S(2)}) collective-permute-start(bf16[128,2048]{1,0:T(8,128)(2,1)} %collective-permute-done.15.refs_3_), channel_id=1, source_target_pairs={{0,96},{16,112},{32,0},{48,16},{64,32},{80,48},{96,64},{112,80},{1... | collective-permute-start | bytes 1572872 | tf_op jit(solution)/shard_map/gather_cycle/ppermute | solution.py:317
  140.5 35.0 %all-to-all-start.3 = ((bf16[16,512,128]{2,1,0:T(8,128)(2,1)}), bf16[16,512,128]{2,1,0:T(8,128)(2,1)}, u32[]{:S(2)}, u32[]{:S(2)}) async-start(bf16[16,512,128]{2,1,0:T(8,128)(2,1)} %half_ladder.3), calls=%async_computation.3 | async-start | bytes 4194304 | tf_op jit(solution)/shard_map/half_ladder/all_to_all | solution.py:366
  147.6 4.4 %collective-permute-start.23 = (bf16[128,2048]{1,0:T(8,128)(2,1)}, bf16[128,2048]{1,0:T(8,128)(2,1)}, u32[]{:S(2)}, u32[]{:S(2)}) collective-permute-start(bf16[128,2048]{1,0:T(8,128)(2,1)} %collective-permute-done.15.refs_3_), channel_id=1, source_target_pairs={{0,16},{16,0},{32,48},{48,32},{64,80},{80,64},{96,112},{112,96},{1... | collective-permute-start | bytes 1572872 | tf_op jit(solution)/shard_map/gather_cycle/ppermute | solution.py:320
  147.7 5.0 %collective-permute-start.24 = (bf16[128,2048]{1,0:T(8,128)(2,1)}, bf16[128,2048]{1,0:T(8,128)(2,1)}, u32[]{:S(2)}, u32[]{:S(2)}) collective-permute-start(bf16[128,2048]{1,0:T(8,128)(2,1)} %collective-permute-done.16.refs_4_), channel_id=1, source_target_pairs={{0,16},{16,0},{32,48},{48,32},{64,80},{80,64},{96,112},{112,96},{1... | collective-permute-start | bytes 1572872 | tf_op jit(solution)/shard_map/gather_cycle/ppermute | solution.py:320
  (27 other events, 550.6 us)

commit v3 on v2

--- a/solution.py
+++ b/solution.py
@@ -61,24 +61,31 @@
     return (len(parts) // 2, 2 * rows, columns)
 
 
-def split_kernel(a_ref, out_ref):
-    pairs, rows, _ = a_ref.shape
-    for v in range(out_ref.shape[0]):
-        out_ref[v] = a_ref[:, :, v * LANES : (v + 1) * LANES].reshape(pairs * rows, LANES)
+def split_kernel(a_ref, out_ref, sems):
+    copies = [
+        pltpu.make_async_copy(a_ref.at[:, :, pl.ds(v * LANES, LANES)], out_ref.at[v], sems.at[v])
+        for v in range(out_ref.shape[0])
+    ]
+    for copy in copies:
+        copy.start()
+    for copy in copies:
+        copy.wait()
 
 
 def split_columns(amplitudes):
     pairs, rows, columns = amplitudes.shape
-    whole = pl.BlockSpec(memory_space=pltpu.VMEM)
-    return pl.pallas_call(
+    owners = columns // LANES
+    blocks = pl.pallas_call(
         split_kernel,
-        in_specs=[whole],
-        out_specs=whole,
-        out_shape=jax.ShapeDtypeStruct((columns // LANES, pairs * rows, LANES), amplitudes.dtype),
+        in_specs=[pl.BlockSpec(memory_space=pltpu.VMEM)],
+        out_specs=pl.BlockSpec(memory_space=pl.ANY),
+        out_shape=pltpu.HBM((owners, pairs, rows, LANES), amplitudes.dtype),
+        scratch_shapes=[pltpu.SemaphoreType.DMA((owners,))],
         compiler_params=params(8),
         cost_estimate=SMALL,
         name="split_columns",
     )(amplitudes)
+    return blocks.reshape(owners, pairs * rows, LANES)
 
 
 def half_kernel(first, place_ref, a_ref, *refs):
@@ -212,6 +219,10 @@
 
 
 HEIGHT = 512
+
+
+def keep_in(space, values):
+    return [pltpu.with_memory_space_constraint(value, space) for value in values]
 
 
 def update_main(pair_energy, cycle_parts, ladder_parts, amps, half, base, screen):
@@ -261,15 +272,15 @@
         grid_spec=grid_spec,
         out_shape=[
             jax.ShapeDtypeStruct((pairs, virt, LANES), jnp.bfloat16),
-            jax.ShapeDtypeStruct(((pairs - count) // 2, virt, 2 * LANES), jnp.float32),
-            jax.ShapeDtypeStruct(panel, jnp.bfloat16),
+            pltpu.HBM(((pairs - count) // 2, virt, 2 * LANES), jnp.float32),
+            pltpu.HBM(panel, jnp.bfloat16),
         ],
-        compiler_params=params(60),
+        compiler_params=params(40),
         cost_estimate=SMALL,
         name="update_main",
     )(
         lax.axis_index("pair").reshape(1), pair_energy, amps, half, base, screen,
-        *cycle_parts, *ladder_parts,
+        *keep_in(pltpu.HBM, cycle_parts), *keep_in(pltpu.HBM, ladder_parts),
     )
 
 
@@ -285,7 +296,7 @@
         in_specs=[
             pl.BlockSpec(memory_space=pltpu.SMEM),
             pl.BlockSpec((height, virt), lambda i: (i, 0)),
-            pl.BlockSpec(half.shape, lambda i: (0, 0, 0)),
+            pl.BlockSpec(memory_space=pltpu.VMEM),
             pl.BlockSpec((count // 2, height, 2 * LANES), lambda i: (0, i, 0)),
             pl.BlockSpec((height, LANES), lambda i: (i, 0)),
             pl.BlockSpec((count, height // TILE, LANES), lambda i: (group, i, 0)),
@@ -295,10 +306,10 @@
         out_shape=jax.ShapeDtypeStruct(previous.shape, previous.dtype),
         scratch_shapes=[pltpu.VMEM((count // 2, virt, 2 * LANES), jnp.bfloat16)],
         input_output_aliases={6: 0},
-        compiler_params=params(60),
+        compiler_params=params(24),
         cost_estimate=SMALL,
         name="update_ladder",
-    )(pair_energy, ladder, half, part, base, screen, previous)
+    )(pair_energy, *keep_in(pltpu.HBM, [ladder]), half, *keep_in(pltpu.HBM, [part]), base, screen, previous)
 
 
 def local(amplitudes, cycle_panel, ladder_panel, virt_energy, pair_energy, tile_mask):

time: 186 us -> 183 us (0.984)
  local copies, waits for them, and re-layouts: 5.99 us -> 2.78 us
  starting transfers between devices: 43.1 us -> 45 us
    all_to_all x1, waiting for transfers between devices: 5.07 us -> 1.67 us  [local(): half = exchange(sent)]
    unnamed x40 -> x50, local copies, waits for them, and re-layouts: 4.2 us -> 1.58 us
  transfers between devices with their start and end apart: 31 -> 31, of which waited for: 12 -> 15; matrix products, arithmetic and copies ran while one was open for 1% -> 1% of each run, Pallas kernels for 22% -> 22%
where the time goes in v3:
time: 183 us
  Pallas kernels  51.8 us (28%)
  waiting for transfers between devices  46.6 us (25%)
  starting transfers between devices  45 us (25%)
  blocking collectives  35 us (19%)
  local copies, waits for them, and re-layouts  2.78 us (2%)
    ppermute x12, waiting for transfers between devices, along(): return lax.ppermute(part, 'pair', z_shift(ranks, step))  38.6 us
    all_to_all x1, blocking collectives, local(): both = exchange(jnp.broadcast_to(both[None], (owners, 2 * rows, columns)))  35 us
    pallas_call x1, Pallas kernels, update_main(): pl.pallas_call(main_kernel, grid_spec=grid_spec, out_shape=[jax.ShapeDtyp...  19.8 us
    pallas_call x2, Pallas kernels, half_ladder(): pl.pallas_call(functools.partial(half_kernel, first), grid=(1,), in_specs...  19.8 us
    ppermute x12, starting transfers between devices, along(): return lax.ppermute(part, 'pair', z_shift(ranks, step))  17.5 us
    ppermute x16, starting transfers between devices, across(): return [lax.ppermute(part, 'pair', other_core(ranks)) for part in parts]  11.8 us
    pallas_call x1, Pallas kernels, update_ladder(): pl.pallas_call(functools.partial(ladder_kernel, first), grid=(virt // hei...  9.88 us
    all_to_all x1, starting transfers between devices, local(): half_tail = exchange(sent)  5.87 us
  transfers between devices with their start and end apart: 31, of which 15 were waited for; matrix products, arithmetic and copies ran while one was open for 1% of the time, Pallas kernels for 22%

profile of v3, /device:TPU:1, one launch (start us, length us, event | category | flops | bytes accessed | tf_op | source)
XLA Modules:
  0.0 182.7 jit_solution(6377532886981958074)
XLA Ops:
  1.1 35.0 %all_to_all.20 = bf16[16,32,2048]{2,1,0:T(8,128)(2,1)S(1)} all-to-all(bf16[16,32,2048]{2,1,0:T(8,128)(2,1)S(1)} %broadcast_in_dim.4), channel_id=1, replica_groups=mesh['pair'=8,'virt'=16] {'virt'}, dimensions={0} | all-to-all | bytes 4194304 | tf_op jit(solution)/shard_map/spread_panels/all_to_all | solution.py:341
  36.5 2.3 %split_columns.1 = bf16[16,8,128,128]{3,2,1,0:T(8,128)(2,1)} custom-call(bf16[8,128,2048]{2,1,0:T(8,128)(2,1)S(1)} %copy-done), custom_call_target="tpu_custom_call" | custom-call | flops 1 | bytes 1 | tf_op jit(solution)/shard_map/exchange_amplitudes/split_columns/pallas_call | solution.py:78
  38.7 4.6 %all-to-all-start.1 = ((bf16[16,1024,128]{2,1,0:T(8,128)(2,1)}), bf16[16,1024,128]{2,1,0:T(8,128)(2,1)}, u32[]{:S(2)}, u32[]{:S(2)}) async-start(bf16[16,1024,128]{2,1,0:T(8,128)(2,1)} %bitcast.7), calls=%async_computation.1 | async-start | bytes 8388608 | tf_op jit(solution)/shard_map/exchange_amplitudes/all_to_all | solution.py:351
  43.3 2.1 %collective-permute-start.2 = (bf16[128,2048]{1,0:T(8,128)(2,1)S(1)}, bf16[128,2048]{1,0:T(8,128)(2,1)S(1)}, u32[]{:S(2)}, u32[]{:S(2)}) collective-permute-start(bf16[128,2048]{1,0:T(8,128)(2,1)S(1)} %bitcast.23), channel_id=1, source_target_pairs={{0,16},{16,0},{32,48},{48,32},{64,80},{80,64},{96,112},{112,96},{1... | collective-permute-start | bytes 1572872 | tf_op jit(solution)/shard_map/gather_ladder/ppermute | solution.py:331
  45.4 1.7 collective-permute-start
  47.4 1.9 %collective-permute-start.1 = (bf16[128,2048]{1,0:T(8,128)(2,1)S(1)}, bf16[128,2048]{1,0:T(8,128)(2,1)S(1)}, u32[]{:S(2)}, u32[]{:S(2)}) collective-permute-start(bf16[128,2048]{1,0:T(8,128)(2,1)S(1)} %bitcast.18), channel_id=1, source_target_pairs={{0,96},{16,112},{32,0},{48,16},{64,32},{80,48},{96,64},{112,80},{1... | collective-permute-start | bytes 1572872 | tf_op jit(solution)/shard_map/gather_ladder/ppermute | solution.py:328
  49.3 1.7 collective-permute-start.5
  51.1 10.4 %collective-permute-done.refs_2_.refs_18_ = bf16[128,2048]{1,0:T(8,128)(2,1)S(1)} collective-permute-done((bf16[128,2048]{1,0:T(8,128)(2,1)S(1)}, bf16[128,2048]{1,0:T(8,128)(2,1)S(1)}, u32[]{:S(2)}, u32[]{:S(2)}) %collective-permute-start) | collective-permute-done | bytes 524320 | tf_op jit(solution)/shard_map/gather_ladder/ppermute | solution.py:328
  62.5 1.7 collective-permute-start.7
  64.2 1.7 collective-permute-start.8
  65.9 6.6 %collective-permute-done.5.refs_5_.refs_21_ = bf16[128,2048]{1,0:T(8,128)(2,1)} collective-permute-done((bf16[128,2048]{1,0:T(8,128)(2,1)S(1)}, bf16[128,2048]{1,0:T(8,128)(2,1)}, u32[]{:S(2)}, u32[]{:S(2)}) %collective-permute-start.5) | collective-permute-done | bytes 524320 | tf_op jit(solution)/shard_map/gather_ladder/ppermute | solution.py:328
  73.6 10.3 %collective-permute-done.6.refs_6_.refs_22_ = bf16[128,2048]{1,0:T(8,128)(2,1)} collective-permute-done((bf16[128,2048]{1,0:T(8,128)(2,1)S(1)}, bf16[128,2048]{1,0:T(8,128)(2,1)}, u32[]{:S(2)}, u32[]{:S(2)}) %collective-permute-start.6) | collective-permute-done | bytes 524320 | tf_op jit(solution)/shard_map/gather_ladder/ppermute | solution.py:328
  87.5 2.3 %collective-permute-start.15 = (bf16[128,2048]{1,0:T(8,128)(2,1)S(1)}, bf16[128,2048]{1,0:T(8,128)(2,1)}, u32[]{:S(2)}, u32[]{:S(2)}) collective-permute-start(bf16[128,2048]{1,0:T(8,128)(2,1)S(1)} %bitcast.9), channel_id=1, source_target_pairs={{0,96},{16,112},{32,0},{48,16},{64,32},{80,48},{96,64},{112,80},{1... | collective-permute-start | bytes 1572872 | tf_op jit(solution)/shard_map/gather_cycle/ppermute | solution.py:328
  90.8 9.9 %half_ladder.2 = bf16[16,512,128]{2,1,0:T(8,128)(2,1)} custom-call(s32[1]{0:T(128)} %bitcast.place_ref, bf16[8,128,2048]{2,1,0:T(8,128)(2,1)} %a_ref.3, bf16[128,2048]{1,0:T(8,128)(2,1)} %bitcast.26, bf16[128,2048]{1,0:T(8,128)(2,1)} %bitcast.20, bf16[128,2048]{1,0:T(8,128)(2,1)} %copy-done.7, bf16[128,2048]{1,0:T(8,128)(2,1)} %copy-done.9, ...), custom_call_target="tpu_custom_call" | custom-call | flops 4294967296 | bytes 8388608 | tf_op jit(solution)/shard_map/half_ladder/half_ladder/pallas_call | solution.py:116
  102.8 5.2 %all-to-all-start.2 = ((bf16[16,512,128]{2,1,0:T(8,128)(2,1)}), bf16[16,512,128]{2,1,0:T(8,128)(2,1)S(1)}, u32[]{:S(2)}, u32[]{:S(2)}) async-start(bf16[16,512,128]{2,1,0:T(8,128)(2,1)} %half_ladder.2), calls=%async_computation.2 | async-start | bytes 4194304 | tf_op jit(solution)/shard_map/half_ladder/all_to_all | solution.py:370
  108.0 3.1 %collective-permute-start.17 = (bf16[128,2048]{1,0:T(8,128)(2,1)}, bf16[128,2048]{1,0:T(8,128)(2,1)S(1)}, u32[]{:S(2)}, u32[]{:S(2)}) collective-permute-start(bf16[128,2048]{1,0:T(8,128)(2,1)} %bitcast.14), channel_id=1, source_target_pairs={{0,96},{16,112},{32,0},{48,16},{64,32},{80,48},{96,64},{112,80},{1... | collective-permute-start | bytes 1572872 | tf_op jit(solution)/shard_map/gather_cycle/ppermute | solution.py:328
  111.0 2.7 %collective-permute-start.19 = (bf16[128,2048]{1,0:T(8,128)(2,1)}, bf16[128,2048]{1,0:T(8,128)(2,1)}, u32[]{:S(2)}, u32[]{:S(2)}) collective-permute-start(bf16[128,2048]{1,0:T(8,128)(2,1)} %collective-permute-done.15.refs_3_), channel_id=1, source_target_pairs={{0,96},{16,112},{32,0},{48,16},{64,32},{80,48},{96,64},{112,80},{1... | collective-permute-start | bytes 1572872 | tf_op jit(solution)/shard_map/gather_cycle/ppermute | solution.py:328
  113.7 9.9 %half_ladder.3 = bf16[16,512,128]{2,1,0:T(8,128)(2,1)} custom-call(s32[1]{0:T(128)} %bitcast.place_ref, bf16[8,128,2048]{2,1,0:T(8,128)(2,1)} %a_ref.3, bf16[128,2048]{1,0:T(8,128)(2,1)} %bitcast.27, bf16[128,2048]{1,0:T(8,128)(2,1)} %bitcast.21, bf16[128,2048]{1,0:T(8,128)(2,1)} %copy-done.7, bf16[128,2048]{1,0:T(8,128)(2,1)} %copy-done.9, ...), custom_call_target="tpu_custom_call" | custom-call | flops 4294967296 | bytes 8388608 | tf_op jit(solution)/shard_map/half_ladder/half_ladder/pallas_call | solution.py:116
  123.7 10.8 %collective-permute-done.18.refs_6_ = bf16[128,2048]{1,0:T(8,128)(2,1)} collective-permute-done((bf16[128,2048]{1,0:T(8,128)(2,1)}, bf16[128,2048]{1,0:T(8,128)(2,1)}, u32[]{:S(2)}, u32[]{:S(2)}) %collective-permute-start.18) | collective-permute-done | bytes 524320 | tf_op jit(solution)/shard_map/gather_cycle/ppermute | solution.py:328
  134.5 1.7 all-to-all-done.2.h_ref
  136.1 5.9 %all-to-all-start.3 = ((bf16[16,512,128]{2,1,0:T(8,128)(2,1)}), bf16[16,512,128]{2,1,0:T(8,128)(2,1)}, u32[]{:S(2)}, u32[]{:S(2)}) async-start(bf16[16,512,128]{2,1,0:T(8,128)(2,1)} %half_ladder.3), calls=%async_computation.3 | async-start | bytes 4194304 | tf_op jit(solution)/shard_map/half_ladder/all_to_all | solution.py:377
  142.0 3.1 %collective-permute-start.20 = (bf16[128,2048]{1,0:T(8,128)(2,1)}, bf16[128,2048]{1,0:T(8,128)(2,1)S(1)}, u32[]{:S(2)}, u32[]{:S(2)}) collective-permute-start(bf16[128,2048]{1,0:T(8,128)(2,1)} %bitcast.15), channel_id=1, source_target_pairs={{0,16},{16,0},{32,48},{48,32},{64,80},{80,64},{96,112},{112,96},{1... | collective-permute-start | bytes 1572872 | tf_op jit(solution)/shard_map/gather_cycle/ppermute | solution.py:331
  153.0 19.8 %update_main.1 = (bf16[8,2048,128]{2,1,0:T(8,128)(2,1)}, f32[2,2048,256]{2,1,0:T(8,128)}, bf16[8,256,2048]{2,1,0:T(8,128)(2,1)}) custom-call(s32[1]{0:T(128)} %bitcast.place_ref, f32[8]{0:T(128)S(1)} %copy-done.1, bf16[16,1024,128]{2,1,0:T(8,128)(2,1)} %all-to-all-done.1.a_ref, bf16[16,512,128]{2,1,0:T(8,128)(2,1)S(1)} %all-to-all-done.2.h_ref, ...), custom_call_target="tpu_custom_call" | custom-call | flops 1 | bytes 1 | tf_op jit(solution)/shard_map/update/update_main/pallas_call | solution.py:270
  172.9 9.9 %update_ladder.1 = bf16[8,2048,128]{2,1,0:T(8,128)(2,1)} custom-call(f32[8]{0:T(128)S(1)} %copy-done.1, bf16[2048,2048]{1,0:T(8,128)(2,1)} %bitcast.8, bf16[16,512,128]{2,1,0:T(8,128)(2,1)} %all-to-all-done.3.h_ref, f32[2,2048,256]{2,1,0:T(8,128)} %get-tuple-element.67.part_ref, ...), custom_call_target="tpu_custom_call", output_to_operand_aliasing={{}: (6, {})} | custom-call | flops 1 | bytes 1 | tf_op jit(solution)/shard_map/update/update_ladder/pallas_call | solution.py:293
  (103 shorter events, 18.3 us)
Async XLA Ops:
  38.7 64.0 %all-to-all-start.1 = ((bf16[16,1024,128]{2,1,0:T(8,128)(2,1)}), bf16[16,1024,128]{2,1,0:T(8,128)(2,1)}, u32[]{:S(2)}, u32[]{:S(2)}) async-start(bf16[16,1024,128]{2,1,0:T(8,128)(2,1)} %bitcast.7), calls=%async_computation.1 | async-start | bytes 8388608 | tf_op jit(solution)/shard_map/exchange_amplitudes/all_to_all | solution.py:351
  43.3 7.7 %collective-permute-start.2 = (bf16[128,2048]{1,0:T(8,128)(2,1)S(1)}, bf16[128,2048]{1,0:T(8,128)(2,1)S(1)}, u32[]{:S(2)}, u32[]{:S(2)}) collective-permute-start(bf16[128,2048]{1,0:T(8,128)(2,1)S(1)} %bitcast.23), channel_id=1, source_target_pairs={{0,16},{16,0},{32,48},{48,32},{64,80},{80,64},{96,112},{112,96},{1... | collective-permute-start | bytes 1572872 | tf_op jit(solution)/shard_map/gather_ladder/ppermute | solution.py:331
  45.4 16.1 %collective-permute-start = (bf16[128,2048]{1,0:T(8,128)(2,1)S(1)}, bf16[128,2048]{1,0:T(8,128)(2,1)S(1)}, u32[]{:S(2)}, u32[]{:S(2)}) collective-permute-start(bf16[128,2048]{1,0:T(8,128)(2,1)S(1)} %bitcast.24), channel_id=1, source_target_pairs={{0,32},{16,48},{32,64},{48,80},{64,96},{80,112},{96,0},{112,16},{1... | collective-permute-start | bytes 1572872 | tf_op jit(solution)/shard_map/gather_ladder/ppermute | solution.py:328
  47.0 14.4 %collective-permute-start.3 = (bf16[128,2048]{1,0:T(8,128)(2,1)S(1)}, bf16[128,2048]{1,0:T(8,128)(2,1)S(1)}, u32[]{:S(2)}, u32[]{:S(2)}) collective-permute-start(bf16[128,2048]{1,0:T(8,128)(2,1)S(1)} %bitcast.17), channel_id=1, source_target_pairs={{0,16},{16,0},{32,48},{48,32},{64,80},{80,64},{96,112},{112,96},{1... | collective-permute-start | bytes 1572872 | tf_op jit(solution)/shard_map/gather_ladder/ppermute | solution.py:331
  47.4 14.1 %collective-permute-start.1 = (bf16[128,2048]{1,0:T(8,128)(2,1)S(1)}, bf16[128,2048]{1,0:T(8,128)(2,1)S(1)}, u32[]{:S(2)}, u32[]{:S(2)}) collective-permute-start(bf16[128,2048]{1,0:T(8,128)(2,1)S(1)} %bitcast.18), channel_id=1, source_target_pairs={{0,96},{16,112},{32,0},{48,16},{64,32},{80,48},{96,64},{112,80},{1... | collective-permute-start | bytes 1572872 | tf_op jit(solution)/shard_map/gather_ladder/ppermute | solution.py:328
  49.3 23.2 %collective-permute-start.5 = (bf16[128,2048]{1,0:T(8,128)(2,1)S(1)}, bf16[128,2048]{1,0:T(8,128)(2,1)}, u32[]{:S(2)}, u32[]{:S(2)}) collective-permute-start(bf16[128,2048]{1,0:T(8,128)(2,1)S(1)} %bitcast.25), channel_id=1, source_target_pairs={{0,96},{16,112},{32,0},{48,16},{64,32},{80,48},{96,64},{112,80},{1... | collective-permute-start | bytes 1572872 | tf_op jit(solution)/shard_map/gather_ladder/ppermute | solution.py:328
  51.0 22.6 %collective-permute-start.4 = (bf16[128,2048]{1,0:T(8,128)(2,1)S(1)}, bf16[128,2048]{1,0:T(8,128)(2,1)S(1)}, u32[]{:S(2)}, u32[]{:S(2)}) collective-permute-start(bf16[128,2048]{1,0:T(8,128)(2,1)S(1)} %bitcast.19), channel_id=1, source_target_pairs={{0,32},{16,48},{32,64},{48,80},{64,96},{80,112},{96,0},{112,16},{1... | collective-permute-start | bytes 1572872 | tf_op jit(solution)/shard_map/gather_ladder/ppermute | solution.py:328
  61.5 22.4 %collective-permute-start.6 = (bf16[128,2048]{1,0:T(8,128)(2,1)S(1)}, bf16[128,2048]{1,0:T(8,128)(2,1)}, u32[]{:S(2)}, u32[]{:S(2)}) collective-permute-start(bf16[128,2048]{1,0:T(8,128)(2,1)S(1)} %collective-permute-done.refs_2_.refs_18_), channel_id=1, source_target_pairs={{0,32},{16,48},{32,64},{48,80},{64,96},{80,112},{96,0},{112,16},{1... | collective-permute-start | bytes 1572872 | tf_op jit(solution)/shard_map/gather_ladder/ppermute | solution.py:328
  62.5 21.4 %collective-permute-start.7 = (bf16[128,2048]{1,0:T(8,128)(2,1)S(1)}, bf16[128,2048]{1,0:T(8,128)(2,1)}, u32[]{:S(2)}, u32[]{:S(2)}) collective-permute-start(bf16[128,2048]{1,0:T(8,128)(2,1)S(1)} %collective-permute-done.1.refs_3_.refs_19_), channel_id=1, source_target_pairs={{0,96},{16,112},{32,0},{48,16},{64,32},{80,48},{96,64},{112,80},{1... | collective-permute-start | bytes 1572872 | tf_op jit(solution)/shard_map/gather_ladder/ppermute | solution.py:328
  64.2 20.9 %collective-permute-start.8 = (bf16[128,2048]{1,0:T(8,128)(2,1)S(1)}, bf16[128,2048]{1,0:T(8,128)(2,1)S(1)}, u32[]{:S(2)}, u32[]{:S(2)}) collective-permute-start(bf16[128,2048]{1,0:T(8,128)(2,1)S(1)} %collective-permute-done.refs_2_.refs_18_), channel_id=1, source_target_pairs={{0,16},{16,0},{32,48},{48,32},{64,80},{80,64},{96,112},{112,96},{1... | collective-permute-start | bytes 1572872 | tf_op jit(solution)/shard_map/gather_ladder/ppermute | solution.py:331
  72.5 13.5 %collective-permute-start.9 = (bf16[128,2048]{1,0:T(8,128)(2,1)S(1)}, bf16[128,2048]{1,0:T(8,128)(2,1)S(1)}, u32[]{:S(2)}, u32[]{:S(2)}) collective-permute-start(bf16[128,2048]{1,0:T(8,128)(2,1)S(1)} %collective-permute-done.1.refs_3_.refs_19_), channel_id=1, source_target_pairs={{0,16},{16,0},{32,48},{48,32},{64,80},{80,64},{96,112},{112,96},{1... | collective-permute-start | bytes 1572872 | tf_op jit(solution)/shard_map/gather_ladder/ppermute | solution.py:331
  84.6 6.2 %collective-permute-start.11 = (bf16[128,2048]{1,0:T(8,128)(2,1)}, bf16[128,2048]{1,0:T(8,128)(2,1)}, u32[]{:S(2)}, u32[]{:S(2)}) collective-permute-start(bf16[128,2048]{1,0:T(8,128)(2,1)} %collective-permute-done.5.refs_5_.refs_21_), channel_id=1, source_target_pairs={{0,16},{16,0},{32,48},{48,32},{64,80},{80,64},{96,112},{112,96},{1... | collective-permute-start | bytes 1572872 | tf_op jit(solution)/shard_map/gather_ladder/ppermute | solution.py:331
  84.7 6.1 %collective-permute-start.12 = (bf16[128,2048]{1,0:T(8,128)(2,1)}, bf16[128,2048]{1,0:T(8,128)(2,1)}, u32[]{:S(2)}, u32[]{:S(2)}) collective-permute-start(bf16[128,2048]{1,0:T(8,128)(2,1)} %collective-permute-done.6.refs_6_.refs_22_), channel_id=1, source_target_pairs={{0,16},{16,0},{32,48},{48,32},{64,80},{80,64},{96,112},{112,96},{1... | collective-permute-start | bytes 1572872 | tf_op jit(solution)/shard_map/gather_ladder/ppermute | solution.py:331
  85.1 5.7 %collective-permute-start.13 = (bf16[128,2048]{1,0:T(8,128)(2,1)}, bf16[128,2048]{1,0:T(8,128)(2,1)}, u32[]{:S(2)}, u32[]{:S(2)}) collective-permute-start(bf16[128,2048]{1,0:T(8,128)(2,1)} %collective-permute-done.7.refs_7_.refs_23_), channel_id=1, source_target_pairs={{0,16},{16,0},{32,48},{48,32},{64,80},{80,64},{96,112},{112,96},{1... | collective-permute-start | bytes 1572872 | tf_op jit(solution)/shard_map/gather_ladder/ppermute | solution.py:331
  86.0 15.2 %collective-permute-start.14 = (bf16[128,2048]{1,0:T(8,128)(2,1)S(1)}, bf16[128,2048]{1,0:T(8,128)(2,1)}, u32[]{:S(2)}, u32[]{:S(2)}) collective-permute-start(bf16[128,2048]{1,0:T(8,128)(2,1)S(1)} %bitcast.13), channel_id=1, source_target_pairs={{0,32},{16,48},{32,64},{48,80},{64,96},{80,112},{96,0},{112,16},{1... | collective-permute-start | bytes 1572872 | tf_op jit(solution)/shard_map/gather_cycle/ppermute | solution.py:328
  87.5 13.8 %collective-permute-start.15 = (bf16[128,2048]{1,0:T(8,128)(2,1)S(1)}, bf16[128,2048]{1,0:T(8,128)(2,1)}, u32[]{:S(2)}, u32[]{:S(2)}) collective-permute-start(bf16[128,2048]{1,0:T(8,128)(2,1)S(1)} %bitcast.9), channel_id=1, source_target_pairs={{0,96},{16,112},{32,0},{48,16},{64,32},{80,48},{96,64},{112,80},{1... | collective-permute-start | bytes 1572872 | tf_op jit(solution)/shard_map/gather_cycle/ppermute | solution.py:328
  102.8 33.4 %all-to-all-start.2 = ((bf16[16,512,128]{2,1,0:T(8,128)(2,1)}), bf16[16,512,128]{2,1,0:T(8,128)(2,1)S(1)}, u32[]{:S(2)}, u32[]{:S(2)}) async-start(bf16[16,512,128]{2,1,0:T(8,128)(2,1)} %half_ladder.2), calls=%async_computation.2 | async-start | bytes 4194304 | tf_op jit(solution)/shard_map/half_ladder/all_to_all | solution.py:370
  108.0 15.7 %collective-permute-start.17 = (bf16[128,2048]{1,0:T(8,128)(2,1)}, bf16[128,2048]{1,0:T(8,128)(2,1)S(1)}, u32[]{:S(2)}, u32[]{:S(2)}) collective-permute-start(bf16[128,2048]{1,0:T(8,128)(2,1)} %bitcast.14), channel_id=1, source_target_pairs={{0,96},{16,112},{32,0},{48,16},{64,32},{80,48},{96,64},{112,80},{1... | collective-permute-start | bytes 1572872 | tf_op jit(solution)/shard_map/gather_cycle/ppermute | solution.py:328
  111.0 12.7 %collective-permute-start.16 = (bf16[128,2048]{1,0:T(8,128)(2,1)}, bf16[128,2048]{1,0:T(8,128)(2,1)}, u32[]{:S(2)}, u32[]{:S(2)}) collective-permute-start(bf16[128,2048]{1,0:T(8,128)(2,1)} %bitcast.10), channel_id=1, source_target_pairs={{0,32},{16,48},{32,64},{48,80},{64,96},{80,112},{96,0},{112,16},{1... | collective-permute-start | bytes 1572872 | tf_op jit(solution)/shard_map/gather_cycle/ppermute | solution.py:328
  111.0 23.4 %collective-permute-start.18 = (bf16[128,2048]{1,0:T(8,128)(2,1)}, bf16[128,2048]{1,0:T(8,128)(2,1)}, u32[]{:S(2)}, u32[]{:S(2)}) collective-permute-start(bf16[128,2048]{1,0:T(8,128)(2,1)} %collective-permute-done.14.refs_2_), channel_id=1, source_target_pairs={{0,32},{16,48},{32,64},{48,80},{64,96},{80,112},{96,0},{112,16},{1... | collective-permute-start | bytes 1572872 | tf_op jit(solution)/shard_map/gather_cycle/ppermute | solution.py:328
  111.0 23.4 %collective-permute-start.19 = (bf16[128,2048]{1,0:T(8,128)(2,1)}, bf16[128,2048]{1,0:T(8,128)(2,1)}, u32[]{:S(2)}, u32[]{:S(2)}) collective-permute-start(bf16[128,2048]{1,0:T(8,128)(2,1)} %collective-permute-done.15.refs_3_), channel_id=1, source_target_pairs={{0,96},{16,112},{32,0},{48,16},{64,32},{80,48},{96,64},{112,80},{1... | collective-permute-start | bytes 1572872 | tf_op jit(solution)/shard_map/gather_cycle/ppermute | solution.py:328
  136.1 36.7 %all-to-all-start.3 = ((bf16[16,512,128]{2,1,0:T(8,128)(2,1)}), bf16[16,512,128]{2,1,0:T(8,128)(2,1)}, u32[]{:S(2)}, u32[]{:S(2)}) async-start(bf16[16,512,128]{2,1,0:T(8,128)(2,1)} %half_ladder.3), calls=%async_computation.3 | async-start | bytes 4194304 | tf_op jit(solution)/shard_map/half_ladder/all_to_all | solution.py:377
  142.0 4.9 %collective-permute-start.20 = (bf16[128,2048]{1,0:T(8,128)(2,1)}, bf16[128,2048]{1,0:T(8,128)(2,1)S(1)}, u32[]{:S(2)}, u32[]{:S(2)}) collective-permute-start(bf16[128,2048]{1,0:T(8,128)(2,1)} %bitcast.15), channel_id=1, source_target_pairs={{0,16},{16,0},{32,48},{48,32},{64,80},{80,64},{96,112},{112,96},{1... | collective-permute-start | bytes 1572872 | tf_op jit(solution)/shard_map/gather_cycle/ppermute | solution.py:331
  145.8 4.1 %collective-permute-start.24 = (bf16[128,2048]{1,0:T(8,128)(2,1)}, bf16[128,2048]{1,0:T(8,128)(2,1)S(1)}, u32[]{:S(2)}, u32[]{:S(2)}) collective-permute-start(bf16[128,2048]{1,0:T(8,128)(2,1)} %collective-permute-done.16.refs_4_), channel_id=1, source_target_pairs={{0,16},{16,0},{32,48},{48,32},{64,80},{80,64},{96,112},{112,96},{1... | collective-permute-start | bytes 1572872 | tf_op jit(solution)/shard_map/gather_cycle/ppermute | solution.py:331
  (32 other events, 464.8 us)

commit v4 on v3

--- a/solution.py
+++ b/solution.py
@@ -206,16 +206,50 @@
             store(owner).wait()
 
 
-def ladder_kernel(first, energy_ref, l_ref, h_ref, part_ref, base_ref, screen_ref, previous_ref, out_ref, h_wide):
+def ladder_kernel(
+    first, cuts, energy_ref, l_hbm, h_ref, part_hbm, base_hbm, screen_ref, previous_ref, out_hbm,
+    l_ref, part_ref, base_ref, out_ref, h_wide, sems, out_done,
+):
     del previous_ref
-
-    @pl.when(pl.program_id(0) == 0)
-    def _():
-        widen(h_ref, h_wide)
-
-    for q in range(h_wide.shape[0]):
-        total = part_ref[q] + jnp.dot(l_ref[...], h_wide[q], preferred_element_type=jnp.float32)
-        finish(first, total, q, energy_ref, base_ref, screen_ref, out_ref)
+    count = out_ref.shape[0]
+    spans = [pl.ds(low, high - low) for low, high in zip(cuts, cuts[1:])]
+
+    def loads(i):
+        rows = spans[i]
+        return [
+            pltpu.make_async_copy(l_hbm.at[rows], l_ref.at[rows], sems.at[i, 0]),
+            pltpu.make_async_copy(part_hbm.at[:, rows], part_ref.at[:, rows], sems.at[i, 1]),
+            pltpu.make_async_copy(base_hbm.at[rows], base_ref.at[rows], sems.at[i, 2]),
+        ]
+
+    def store(i):
+        rows = spans[i]
+        return pltpu.make_async_copy(
+            out_ref.at[:, rows], out_hbm.at[pl.ds(first, count), rows], out_done.at[i]
+        )
+
+    for i in range(2):
+        for load in loads(i):
+            load.start()
+    widen(h_ref, h_wide)
+    for i, rows in enumerate(spans):
+        for load in loads(i):
+            load.wait()
+        if i + 2 < len(spans):
+            for load in loads(i + 2):
+                load.start()
+        tiles = pl.ds(rows.start // TILE, rows.size // TILE)
+        for q in range(h_wide.shape[0]):
+            total = part_ref[q, rows] + jnp.dot(
+                l_ref[rows], h_wide[q], preferred_element_type=jnp.float32
+            )
+            finish(
+                first, total, q, energy_ref, base_ref.at[rows],
+                screen_ref.at[pl.ds(first, count), tiles], out_ref.at[:, rows],
+            )
+        store(i).start()
+    for i in range(len(spans)):
+        store(i).wait()
 
 
 HEIGHT = 512
@@ -288,28 +322,40 @@
     owners = half.shape[0]
     virt = ladder.shape[0]
     count = half.shape[1] // (virt // owners)
-    group = first // count
-    height = HEIGHT
+    cuts = (0, HEIGHT // 2, *range(3 * HEIGHT // 2, virt, HEIGHT), virt)
+    steps = len(cuts) - 1
+    anywhere = pl.BlockSpec(memory_space=pl.ANY)
+    whole = pl.BlockSpec(memory_space=pltpu.VMEM)
     return pl.pallas_call(
-        functools.partial(ladder_kernel, first),
-        grid=(virt // height,),
+        functools.partial(ladder_kernel, first, cuts),
         in_specs=[
             pl.BlockSpec(memory_space=pltpu.SMEM),
-            pl.BlockSpec((height, virt), lambda i: (i, 0)),
-            pl.BlockSpec(memory_space=pltpu.VMEM),
-            pl.BlockSpec((count // 2, height, 2 * LANES), lambda i: (0, i, 0)),
-            pl.BlockSpec((height, LANES), lambda i: (i, 0)),
-            pl.BlockSpec((count, height // TILE, LANES), lambda i: (group, i, 0)),
-            pl.BlockSpec(memory_space=pl.ANY),
+            anywhere,
+            whole,
+            anywhere,
+            anywhere,
+            whole,
+            anywhere,
         ],
-        out_specs=pl.BlockSpec((count, height, LANES), lambda i: (group, i, 0)),
+        out_specs=anywhere,
         out_shape=jax.ShapeDtypeStruct(previous.shape, previous.dtype),
-        scratch_shapes=[pltpu.VMEM((count // 2, virt, 2 * LANES), jnp.bfloat16)],
+        scratch_shapes=[
+            pltpu.VMEM(ladder.shape, jnp.bfloat16),
+            pltpu.VMEM(part.shape, jnp.float32),
+            pltpu.VMEM(base.shape, jnp.float32),
+            pltpu.VMEM((count, virt, LANES), jnp.bfloat16),
+            pltpu.VMEM((count // 2, virt, 2 * LANES), jnp.bfloat16),
+            pltpu.SemaphoreType.DMA((steps, 3)),
+            pltpu.SemaphoreType.DMA((steps,)),
+        ],
         input_output_aliases={6: 0},
-        compiler_params=params(24),
+        compiler_params=params(28),
         cost_estimate=SMALL,
         name="update_ladder",
-    )(pair_energy, *keep_in(pltpu.HBM, [ladder]), half, *keep_in(pltpu.HBM, [part]), base, screen, previous)
+    )(
+        pair_energy, *keep_in(pltpu.HBM, [ladder]), half, *keep_in(pltpu.HBM, [part]), base, screen,
+        previous,
+    )
 
 
 def local(amplitudes, cycle_panel, ladder_panel, virt_energy, pair_energy, tile_mask):

time: 183 us -> 183 us (level)
  no operation moved by 1% of the time
where the time goes in v4:
time: 183 us
  Pallas kernels  51.5 us (28%)
  waiting for transfers between devices  46.6 us (25%)
  starting transfers between devices  45 us (25%)
  blocking collectives  35 us (19%)
  local copies, waits for them, and re-layouts  2.78 us (2%)
    ppermute x12, waiting for transfers between devices, along(): return lax.ppermute(part, 'pair', z_shift(ranks, step))  38.5 us
    all_to_all x1, blocking collectives, local(): both = exchange(jnp.broadcast_to(both[None], (owners, 2 * rows, columns)))  35 us
    pallas_call x2, Pallas kernels, half_ladder(): pl.pallas_call(functools.partial(half_kernel, first), grid=(1,), in_specs...  19.8 us
    pallas_call x1, Pallas kernels, update_main(): pl.pallas_call(main_kernel, grid_spec=grid_spec, out_shape=[jax.ShapeDtyp...  19.8 us
    ppermute x12, starting transfers between devices, along(): return lax.ppermute(part, 'pair', z_shift(ranks, step))  17.5 us
    ppermute x16, starting transfers between devices, across(): return [lax.ppermute(part, 'pair', other_core(ranks)) for part in parts]  11.8 us
    pallas_call x1, Pallas kernels, update_ladder(): pl.pallas_call(functools.partial(ladder_kernel, first, cuts), in_specs=[p...  9.59 us
    all_to_all x1, starting transfers between devices, local(): half_tail = exchange(sent)  5.87 us
  transfers between devices with their start and end apart: 31, of which 15 were waited for; matrix products, arithmetic and copies ran while one was open for 1% of the time, Pallas kernels for 22%

profile of v4, /device:TPU:1, one launch (start us, length us, event | category | flops | bytes accessed | tf_op | source)
XLA Modules:
  0.0 182.6 jit_solution(12132777432480900411)
XLA Ops:
  1.1 35.0 %all_to_all.20 = bf16[16,32,2048]{2,1,0:T(8,128)(2,1)S(1)} all-to-all(bf16[16,32,2048]{2,1,0:T(8,128)(2,1)S(1)} %broadcast_in_dim.4), channel_id=1, replica_groups=mesh['pair'=8,'virt'=16] {'virt'}, dimensions={0} | all-to-all | bytes 4194304 | tf_op jit(solution)/shard_map/spread_panels/all_to_all | solution.py:387
  36.5 2.2 %split_columns.1 = bf16[16,8,128,128]{3,2,1,0:T(8,128)(2,1)} custom-call(bf16[8,128,2048]{2,1,0:T(8,128)(2,1)S(1)} %copy-done), custom_call_target="tpu_custom_call" | custom-call | flops 1 | bytes 1 | tf_op jit(solution)/shard_map/exchange_amplitudes/split_columns/pallas_call | solution.py:78
  38.7 4.6 %all-to-all-start.1 = ((bf16[16,1024,128]{2,1,0:T(8,128)(2,1)}), bf16[16,1024,128]{2,1,0:T(8,128)(2,1)}, u32[]{:S(2)}, u32[]{:S(2)}) async-start(bf16[16,1024,128]{2,1,0:T(8,128)(2,1)} %bitcast.7), calls=%async_computation.1 | async-start | bytes 8388608 | tf_op jit(solution)/shard_map/exchange_amplitudes/all_to_all | solution.py:397
  43.3 2.1 %collective-permute-start.2 = (bf16[128,2048]{1,0:T(8,128)(2,1)S(1)}, bf16[128,2048]{1,0:T(8,128)(2,1)S(1)}, u32[]{:S(2)}, u32[]{:S(2)}) collective-permute-start(bf16[128,2048]{1,0:T(8,128)(2,1)S(1)} %bitcast.23), channel_id=1, source_target_pairs={{0,16},{16,0},{32,48},{48,32},{64,80},{80,64},{96,112},{112,96},{1... | collective-permute-start | bytes 1572872 | tf_op jit(solution)/shard_map/gather_ladder/ppermute | solution.py:377
  45.4 1.7 collective-permute-start
  47.4 1.9 %collective-permute-start.1 = (bf16[128,2048]{1,0:T(8,128)(2,1)S(1)}, bf16[128,2048]{1,0:T(8,128)(2,1)S(1)}, u32[]{:S(2)}, u32[]{:S(2)}) collective-permute-start(bf16[128,2048]{1,0:T(8,128)(2,1)S(1)} %bitcast.18), channel_id=1, source_target_pairs={{0,96},{16,112},{32,0},{48,16},{64,32},{80,48},{96,64},{112,80},{1... | collective-permute-start | bytes 1572872 | tf_op jit(solution)/shard_map/gather_ladder/ppermute | solution.py:374
  49.3 1.7 collective-permute-start.5
  51.0 10.4 %collective-permute-done.refs_2_.refs_18_ = bf16[128,2048]{1,0:T(8,128)(2,1)S(1)} collective-permute-done((bf16[128,2048]{1,0:T(8,128)(2,1)S(1)}, bf16[128,2048]{1,0:T(8,128)(2,1)S(1)}, u32[]{:S(2)}, u32[]{:S(2)}) %collective-permute-start) | collective-permute-done | bytes 524320 | tf_op jit(solution)/shard_map/gather_ladder/ppermute | solution.py:374
  62.5 1.7 collective-permute-start.7
  64.2 1.7 collective-permute-start.8
  65.9 6.6 %collective-permute-done.5.refs_5_.refs_21_ = bf16[128,2048]{1,0:T(8,128)(2,1)} collective-permute-done((bf16[128,2048]{1,0:T(8,128)(2,1)S(1)}, bf16[128,2048]{1,0:T(8,128)(2,1)}, u32[]{:S(2)}, u32[]{:S(2)}) %collective-permute-start.5) | collective-permute-done | bytes 524320 | tf_op jit(solution)/shard_map/gather_ladder/ppermute | solution.py:374
  73.6 10.3 %collective-permute-done.6.refs_6_.refs_22_ = bf16[128,2048]{1,0:T(8,128)(2,1)} collective-permute-done((bf16[128,2048]{1,0:T(8,128)(2,1)S(1)}, bf16[128,2048]{1,0:T(8,128)(2,1)}, u32[]{:S(2)}, u32[]{:S(2)}) %collective-permute-start.6) | collective-permute-done | bytes 524320 | tf_op jit(solution)/shard_map/gather_ladder/ppermute | solution.py:374
  87.4 2.3 %collective-permute-start.15 = (bf16[128,2048]{1,0:T(8,128)(2,1)S(1)}, bf16[128,2048]{1,0:T(8,128)(2,1)}, u32[]{:S(2)}, u32[]{:S(2)}) collective-permute-start(bf16[128,2048]{1,0:T(8,128)(2,1)S(1)} %bitcast.9), channel_id=1, source_target_pairs={{0,96},{16,112},{32,0},{48,16},{64,32},{80,48},{96,64},{112,80},{1... | collective-permute-start | bytes 1572872 | tf_op jit(solution)/shard_map/gather_cycle/ppermute | solution.py:374
  90.8 9.9 %half_ladder.2 = bf16[16,512,128]{2,1,0:T(8,128)(2,1)} custom-call(s32[1]{0:T(128)} %bitcast.place_ref, bf16[8,128,2048]{2,1,0:T(8,128)(2,1)} %a_ref.3, bf16[128,2048]{1,0:T(8,128)(2,1)} %bitcast.26, bf16[128,2048]{1,0:T(8,128)(2,1)} %bitcast.20, bf16[128,2048]{1,0:T(8,128)(2,1)} %copy-done.7, bf16[128,2048]{1,0:T(8,128)(2,1)} %copy-done.9, ...), custom_call_target="tpu_custom_call" | custom-call | flops 4294967296 | bytes 8388608 | tf_op jit(solution)/shard_map/half_ladder/half_ladder/pallas_call | solution.py:116
  102.7 5.2 %all-to-all-start.2 = ((bf16[16,512,128]{2,1,0:T(8,128)(2,1)}), bf16[16,512,128]{2,1,0:T(8,128)(2,1)S(1)}, u32[]{:S(2)}, u32[]{:S(2)}) async-start(bf16[16,512,128]{2,1,0:T(8,128)(2,1)} %half_ladder.2), calls=%async_computation.2 | async-start | bytes 4194304 | tf_op jit(solution)/shard_map/half_ladder/all_to_all | solution.py:416
  107.9 3.1 %collective-permute-start.17 = (bf16[128,2048]{1,0:T(8,128)(2,1)}, bf16[128,2048]{1,0:T(8,128)(2,1)S(1)}, u32[]{:S(2)}, u32[]{:S(2)}) collective-permute-start(bf16[128,2048]{1,0:T(8,128)(2,1)} %bitcast.14), channel_id=1, source_target_pairs={{0,96},{16,112},{32,0},{48,16},{64,32},{80,48},{96,64},{112,80},{1... | collective-permute-start | bytes 1572872 | tf_op jit(solution)/shard_map/gather_cycle/ppermute | solution.py:374
  111.0 2.7 %collective-permute-start.19 = (bf16[128,2048]{1,0:T(8,128)(2,1)}, bf16[128,2048]{1,0:T(8,128)(2,1)}, u32[]{:S(2)}, u32[]{:S(2)}) collective-permute-start(bf16[128,2048]{1,0:T(8,128)(2,1)} %collective-permute-done.15.refs_3_), channel_id=1, source_target_pairs={{0,96},{16,112},{32,0},{48,16},{64,32},{80,48},{96,64},{112,80},{1... | collective-permute-start | bytes 1572872 | tf_op jit(solution)/shard_map/gather_cycle/ppermute | solution.py:374
  113.7 9.9 %half_ladder.3 = bf16[16,512,128]{2,1,0:T(8,128)(2,1)} custom-call(s32[1]{0:T(128)} %bitcast.place_ref, bf16[8,128,2048]{2,1,0:T(8,128)(2,1)} %a_ref.3, bf16[128,2048]{1,0:T(8,128)(2,1)} %bitcast.27, bf16[128,2048]{1,0:T(8,128)(2,1)} %bitcast.21, bf16[128,2048]{1,0:T(8,128)(2,1)} %copy-done.7, bf16[128,2048]{1,0:T(8,128)(2,1)} %copy-done.9, ...), custom_call_target="tpu_custom_call" | custom-call | flops 4294967296 | bytes 8388608 | tf_op jit(solution)/shard_map/half_ladder/half_ladder/pallas_call | solution.py:116
  123.7 10.8 %collective-permute-done.18.refs_6_ = bf16[128,2048]{1,0:T(8,128)(2,1)} collective-permute-done((bf16[128,2048]{1,0:T(8,128)(2,1)}, bf16[128,2048]{1,0:T(8,128)(2,1)}, u32[]{:S(2)}, u32[]{:S(2)}) %collective-permute-start.18) | collective-permute-done | bytes 524320 | tf_op jit(solution)/shard_map/gather_cycle/ppermute | solution.py:374
  134.4 1.7 all-to-all-done.2.h_ref
  136.1 5.9 %all-to-all-start.3 = ((bf16[16,512,128]{2,1,0:T(8,128)(2,1)}), bf16[16,512,128]{2,1,0:T(8,128)(2,1)}, u32[]{:S(2)}, u32[]{:S(2)}) async-start(bf16[16,512,128]{2,1,0:T(8,128)(2,1)} %half_ladder.3), calls=%async_computation.3 | async-start | bytes 4194304 | tf_op jit(solution)/shard_map/half_ladder/all_to_all | solution.py:423
  142.0 3.1 %collective-permute-start.20 = (bf16[128,2048]{1,0:T(8,128)(2,1)}, bf16[128,2048]{1,0:T(8,128)(2,1)S(1)}, u32[]{:S(2)}, u32[]{:S(2)}) collective-permute-start(bf16[128,2048]{1,0:T(8,128)(2,1)} %bitcast.15), channel_id=1, source_target_pairs={{0,16},{16,0},{32,48},{48,32},{64,80},{80,64},{96,112},{112,96},{1... | collective-permute-start | bytes 1572872 | tf_op jit(solution)/shard_map/gather_cycle/ppermute | solution.py:377
  153.0 19.8 %update_main.1 = (bf16[8,2048,128]{2,1,0:T(8,128)(2,1)}, f32[2,2048,256]{2,1,0:T(8,128)}, bf16[8,256,2048]{2,1,0:T(8,128)(2,1)}) custom-call(s32[1]{0:T(128)} %bitcast.place_ref, f32[8]{0:T(128)S(1)} %copy-done.1, bf16[16,1024,128]{2,1,0:T(8,128)(2,1)} %all-to-all-done.1.a_ref, bf16[16,512,128]{2,1,0:T(8,128)(2,1)S(1)} %all-to-all-done.2.h_ref, ...), custom_call_target="tpu_custom_call" | custom-call | flops 1 | bytes 1 | tf_op jit(solution)/shard_map/update/update_main/pallas_call | solution.py:304
  172.8 9.6 %update_ladder.1 = bf16[8,2048,128]{2,1,0:T(8,128)(2,1)} custom-call(f32[8]{0:T(128)S(1)} %copy-done.1, bf16[2048,2048]{1,0:T(8,128)(2,1)} %bitcast.8, bf16[16,512,128]{2,1,0:T(8,128)(2,1)} %all-to-all-done.3.h_ref, f32[2,2048,256]{2,1,0:T(8,128)} %get-tuple-element.67.part_hbm, ...), custom_call_target="tpu_custom_call", output_to_operand_aliasing={{}: (6, {})} | custom-call | flops 1 | bytes 1 | tf_op jit(solution)/shard_map/update/update_ladder/pallas_call | solution.py:329
  (103 shorter events, 18.3 us)
Async XLA Ops:
  38.7 64.0 %all-to-all-start.1 = ((bf16[16,1024,128]{2,1,0:T(8,128)(2,1)}), bf16[16,1024,128]{2,1,0:T(8,128)(2,1)}, u32[]{:S(2)}, u32[]{:S(2)}) async-start(bf16[16,1024,128]{2,1,0:T(8,128)(2,1)} %bitcast.7), calls=%async_computation.1 | async-start | bytes 8388608 | tf_op jit(solution)/shard_map/exchange_amplitudes/all_to_all | solution.py:397
  43.3 7.7 %collective-permute-start.2 = (bf16[128,2048]{1,0:T(8,128)(2,1)S(1)}, bf16[128,2048]{1,0:T(8,128)(2,1)S(1)}, u32[]{:S(2)}, u32[]{:S(2)}) collective-permute-start(bf16[128,2048]{1,0:T(8,128)(2,1)S(1)} %bitcast.23), channel_id=1, source_target_pairs={{0,16},{16,0},{32,48},{48,32},{64,80},{80,64},{96,112},{112,96},{1... | collective-permute-start | bytes 1572872 | tf_op jit(solution)/shard_map/gather_ladder/ppermute | solution.py:377
  45.4 16.1 %collective-permute-start = (bf16[128,2048]{1,0:T(8,128)(2,1)S(1)}, bf16[128,2048]{1,0:T(8,128)(2,1)S(1)}, u32[]{:S(2)}, u32[]{:S(2)}) collective-permute-start(bf16[128,2048]{1,0:T(8,128)(2,1)S(1)} %bitcast.24), channel_id=1, source_target_pairs={{0,32},{16,48},{32,64},{48,80},{64,96},{80,112},{96,0},{112,16},{1... | collective-permute-start | bytes 1572872 | tf_op jit(solution)/shard_map/gather_ladder/ppermute | solution.py:374
  47.0 14.4 %collective-permute-start.3 = (bf16[128,2048]{1,0:T(8,128)(2,1)S(1)}, bf16[128,2048]{1,0:T(8,128)(2,1)S(1)}, u32[]{:S(2)}, u32[]{:S(2)}) collective-permute-start(bf16[128,2048]{1,0:T(8,128)(2,1)S(1)} %bitcast.17), channel_id=1, source_target_pairs={{0,16},{16,0},{32,48},{48,32},{64,80},{80,64},{96,112},{112,96},{1... | collective-permute-start | bytes 1572872 | tf_op jit(solution)/shard_map/gather_ladder/ppermute | solution.py:377
  47.4 14.1 %collective-permute-start.1 = (bf16[128,2048]{1,0:T(8,128)(2,1)S(1)}, bf16[128,2048]{1,0:T(8,128)(2,1)S(1)}, u32[]{:S(2)}, u32[]{:S(2)}) collective-permute-start(bf16[128,2048]{1,0:T(8,128)(2,1)S(1)} %bitcast.18), channel_id=1, source_target_pairs={{0,96},{16,112},{32,0},{48,16},{64,32},{80,48},{96,64},{112,80},{1... | collective-permute-start | bytes 1572872 | tf_op jit(solution)/shard_map/gather_ladder/ppermute | solution.py:374
  49.3 23.2 %collective-permute-start.5 = (bf16[128,2048]{1,0:T(8,128)(2,1)S(1)}, bf16[128,2048]{1,0:T(8,128)(2,1)}, u32[]{:S(2)}, u32[]{:S(2)}) collective-permute-start(bf16[128,2048]{1,0:T(8,128)(2,1)S(1)} %bitcast.25), channel_id=1, source_target_pairs={{0,96},{16,112},{32,0},{48,16},{64,32},{80,48},{96,64},{112,80},{1... | collective-permute-start | bytes 1572872 | tf_op jit(solution)/shard_map/gather_ladder/ppermute | solution.py:374
  51.0 22.6 %collective-permute-start.4 = (bf16[128,2048]{1,0:T(8,128)(2,1)S(1)}, bf16[128,2048]{1,0:T(8,128)(2,1)S(1)}, u32[]{:S(2)}, u32[]{:S(2)}) collective-permute-start(bf16[128,2048]{1,0:T(8,128)(2,1)S(1)} %bitcast.19), channel_id=1, source_target_pairs={{0,32},{16,48},{32,64},{48,80},{64,96},{80,112},{96,0},{112,16},{1... | collective-permute-start | bytes 1572872 | tf_op jit(solution)/shard_map/gather_ladder/ppermute | solution.py:374
  61.5 22.4 %collective-permute-start.6 = (bf16[128,2048]{1,0:T(8,128)(2,1)S(1)}, bf16[128,2048]{1,0:T(8,128)(2,1)}, u32[]{:S(2)}, u32[]{:S(2)}) collective-permute-start(bf16[128,2048]{1,0:T(8,128)(2,1)S(1)} %collective-permute-done.refs_2_.refs_18_), channel_id=1, source_target_pairs={{0,32},{16,48},{32,64},{48,80},{64,96},{80,112},{96,0},{112,16},{1... | collective-permute-start | bytes 1572872 | tf_op jit(solution)/shard_map/gather_ladder/ppermute | solution.py:374
  62.5 21.4 %collective-permute-start.7 = (bf16[128,2048]{1,0:T(8,128)(2,1)S(1)}, bf16[128,2048]{1,0:T(8,128)(2,1)}, u32[]{:S(2)}, u32[]{:S(2)}) collective-permute-start(bf16[128,2048]{1,0:T(8,128)(2,1)S(1)} %collective-permute-done.1.refs_3_.refs_19_), channel_id=1, source_target_pairs={{0,96},{16,112},{32,0},{48,16},{64,32},{80,48},{96,64},{112,80},{1... | collective-permute-start | bytes 1572872 | tf_op jit(solution)/shard_map/gather_ladder/ppermute | solution.py:374
  64.2 20.9 %collective-permute-start.8 = (bf16[128,2048]{1,0:T(8,128)(2,1)S(1)}, bf16[128,2048]{1,0:T(8,128)(2,1)S(1)}, u32[]{:S(2)}, u32[]{:S(2)}) collective-permute-start(bf16[128,2048]{1,0:T(8,128)(2,1)S(1)} %collective-permute-done.refs_2_.refs_18_), channel_id=1, source_target_pairs={{0,16},{16,0},{32,48},{48,32},{64,80},{80,64},{96,112},{112,96},{1... | collective-permute-start | bytes 1572872 | tf_op jit(solution)/shard_map/gather_ladder/ppermute | solution.py:377
  72.5 13.5 %collective-permute-start.9 = (bf16[128,2048]{1,0:T(8,128)(2,1)S(1)}, bf16[128,2048]{1,0:T(8,128)(2,1)S(1)}, u32[]{:S(2)}, u32[]{:S(2)}) collective-permute-start(bf16[128,2048]{1,0:T(8,128)(2,1)S(1)} %collective-permute-done.1.refs_3_.refs_19_), channel_id=1, source_target_pairs={{0,16},{16,0},{32,48},{48,32},{64,80},{80,64},{96,112},{112,96},{1... | collective-permute-start | bytes 1572872 | tf_op jit(solution)/shard_map/gather_ladder/ppermute | solution.py:377
  84.6 6.2 %collective-permute-start.11 = (bf16[128,2048]{1,0:T(8,128)(2,1)}, bf16[128,2048]{1,0:T(8,128)(2,1)}, u32[]{:S(2)}, u32[]{:S(2)}) collective-permute-start(bf16[128,2048]{1,0:T(8,128)(2,1)} %collective-permute-done.5.refs_5_.refs_21_), channel_id=1, source_target_pairs={{0,16},{16,0},{32,48},{48,32},{64,80},{80,64},{96,112},{112,96},{1... | collective-permute-start | bytes 1572872 | tf_op jit(solution)/shard_map/gather_ladder/ppermute | solution.py:377
  84.7 6.1 %collective-permute-start.12 = (bf16[128,2048]{1,0:T(8,128)(2,1)}, bf16[128,2048]{1,0:T(8,128)(2,1)}, u32[]{:S(2)}, u32[]{:S(2)}) collective-permute-start(bf16[128,2048]{1,0:T(8,128)(2,1)} %collective-permute-done.6.refs_6_.refs_22_), channel_id=1, source_target_pairs={{0,16},{16,0},{32,48},{48,32},{64,80},{80,64},{96,112},{112,96},{1... | collective-permute-start | bytes 1572872 | tf_op jit(solution)/shard_map/gather_ladder/ppermute | solution.py:377
  85.1 5.7 %collective-permute-start.13 = (bf16[128,2048]{1,0:T(8,128)(2,1)}, bf16[128,2048]{1,0:T(8,128)(2,1)}, u32[]{:S(2)}, u32[]{:S(2)}) collective-permute-start(bf16[128,2048]{1,0:T(8,128)(2,1)} %collective-permute-done.7.refs_7_.refs_23_), channel_id=1, source_target_pairs={{0,16},{16,0},{32,48},{48,32},{64,80},{80,64},{96,112},{112,96},{1... | collective-permute-start | bytes 1572872 | tf_op jit(solution)/shard_map/gather_ladder/ppermute | solution.py:377
  86.0 15.2 %collective-permute-start.14 = (bf16[128,2048]{1,0:T(8,128)(2,1)S(1)}, bf16[128,2048]{1,0:T(8,128)(2,1)}, u32[]{:S(2)}, u32[]{:S(2)}) collective-permute-start(bf16[128,2048]{1,0:T(8,128)(2,1)S(1)} %bitcast.13), channel_id=1, source_target_pairs={{0,32},{16,48},{32,64},{48,80},{64,96},{80,112},{96,0},{112,16},{1... | collective-permute-start | bytes 1572872 | tf_op jit(solution)/shard_map/gather_cycle/ppermute | solution.py:374
  87.4 13.8 %collective-permute-start.15 = (bf16[128,2048]{1,0:T(8,128)(2,1)S(1)}, bf16[128,2048]{1,0:T(8,128)(2,1)}, u32[]{:S(2)}, u32[]{:S(2)}) collective-permute-start(bf16[128,2048]{1,0:T(8,128)(2,1)S(1)} %bitcast.9), channel_id=1, source_target_pairs={{0,96},{16,112},{32,0},{48,16},{64,32},{80,48},{96,64},{112,80},{1... | collective-permute-start | bytes 1572872 | tf_op jit(solution)/shard_map/gather_cycle/ppermute | solution.py:374
  102.7 33.4 %all-to-all-start.2 = ((bf16[16,512,128]{2,1,0:T(8,128)(2,1)}), bf16[16,512,128]{2,1,0:T(8,128)(2,1)S(1)}, u32[]{:S(2)}, u32[]{:S(2)}) async-start(bf16[16,512,128]{2,1,0:T(8,128)(2,1)} %half_ladder.2), calls=%async_computation.2 | async-start | bytes 4194304 | tf_op jit(solution)/shard_map/half_ladder/all_to_all | solution.py:416
  107.9 15.7 %collective-permute-start.17 = (bf16[128,2048]{1,0:T(8,128)(2,1)}, bf16[128,2048]{1,0:T(8,128)(2,1)S(1)}, u32[]{:S(2)}, u32[]{:S(2)}) collective-permute-start(bf16[128,2048]{1,0:T(8,128)(2,1)} %bitcast.14), channel_id=1, source_target_pairs={{0,96},{16,112},{32,0},{48,16},{64,32},{80,48},{96,64},{112,80},{1... | collective-permute-start | bytes 1572872 | tf_op jit(solution)/shard_map/gather_cycle/ppermute | solution.py:374
  111.0 12.7 %collective-permute-start.16 = (bf16[128,2048]{1,0:T(8,128)(2,1)}, bf16[128,2048]{1,0:T(8,128)(2,1)}, u32[]{:S(2)}, u32[]{:S(2)}) collective-permute-start(bf16[128,2048]{1,0:T(8,128)(2,1)} %bitcast.10), channel_id=1, source_target_pairs={{0,32},{16,48},{32,64},{48,80},{64,96},{80,112},{96,0},{112,16},{1... | collective-permute-start | bytes 1572872 | tf_op jit(solution)/shard_map/gather_cycle/ppermute | solution.py:374
  111.0 23.4 %collective-permute-start.18 = (bf16[128,2048]{1,0:T(8,128)(2,1)}, bf16[128,2048]{1,0:T(8,128)(2,1)}, u32[]{:S(2)}, u32[]{:S(2)}) collective-permute-start(bf16[128,2048]{1,0:T(8,128)(2,1)} %collective-permute-done.14.refs_2_), channel_id=1, source_target_pairs={{0,32},{16,48},{32,64},{48,80},{64,96},{80,112},{96,0},{112,16},{1... | collective-permute-start | bytes 1572872 | tf_op jit(solution)/shard_map/gather_cycle/ppermute | solution.py:374
  111.0 23.4 %collective-permute-start.19 = (bf16[128,2048]{1,0:T(8,128)(2,1)}, bf16[128,2048]{1,0:T(8,128)(2,1)}, u32[]{:S(2)}, u32[]{:S(2)}) collective-permute-start(bf16[128,2048]{1,0:T(8,128)(2,1)} %collective-permute-done.15.refs_3_), channel_id=1, source_target_pairs={{0,96},{16,112},{32,0},{48,16},{64,32},{80,48},{96,64},{112,80},{1... | collective-permute-start | bytes 1572872 | tf_op jit(solution)/shard_map/gather_cycle/ppermute | solution.py:374
  136.1 36.7 %all-to-all-start.3 = ((bf16[16,512,128]{2,1,0:T(8,128)(2,1)}), bf16[16,512,128]{2,1,0:T(8,128)(2,1)}, u32[]{:S(2)}, u32[]{:S(2)}) async-start(bf16[16,512,128]{2,1,0:T(8,128)(2,1)} %half_ladder.3), calls=%async_computation.3 | async-start | bytes 4194304 | tf_op jit(solution)/shard_map/half_ladder/all_to_all | solution.py:423
  142.0 4.9 %collective-permute-start.20 = (bf16[128,2048]{1,0:T(8,128)(2,1)}, bf16[128,2048]{1,0:T(8,128)(2,1)S(1)}, u32[]{:S(2)}, u32[]{:S(2)}) collective-permute-start(bf16[128,2048]{1,0:T(8,128)(2,1)} %bitcast.15), channel_id=1, source_target_pairs={{0,16},{16,0},{32,48},{48,32},{64,80},{80,64},{96,112},{112,96},{1... | collective-permute-start | bytes 1572872 | tf_op jit(solution)/shard_map/gather_cycle/ppermute | solution.py:377
  145.7 4.1 %collective-permute-start.24 = (bf16[128,2048]{1,0:T(8,128)(2,1)}, bf16[128,2048]{1,0:T(8,128)(2,1)S(1)}, u32[]{:S(2)}, u32[]{:S(2)}) collective-permute-start(bf16[128,2048]{1,0:T(8,128)(2,1)} %collective-permute-done.16.refs_4_), channel_id=1, source_target_pairs={{0,16},{16,0},{32,48},{48,32},{64,80},{80,64},{96,112},{112,96},{1... | collective-permute-start | bytes 1572872 | tf_op jit(solution)/shard_map/gather_cycle/ppermute | solution.py:377
  (32 other events, 464.7 us)

commit v5 on v4

--- a/solution.py
+++ b/solution.py
@@ -273,16 +273,13 @@
     def chip(i, place):
         return chip_of(place[0], back_of(i), chips)
 
-    def once(block):
-        return pl.BlockSpec(block.shape, lambda i, place: (0, 0, 0), pipeline_mode=pl.Buffered(1))
-
     grid_spec = pltpu.PrefetchScalarGridSpec(
         num_scalar_prefetch=1,
         grid=(chips,),
         in_specs=[
             pl.BlockSpec(memory_space=pltpu.SMEM),
-            once(amps),
-            once(half),
+            pl.BlockSpec(memory_space=pltpu.VMEM),
+            pl.BlockSpec(memory_space=pltpu.VMEM),
             pl.BlockSpec((HEIGHT, LANES), lambda i, place: (chip(i, place), 0)),
             pl.BlockSpec((count, HEIGHT // TILE, LANES), lambda i, place: (0, chip(i, place), 0)),
         ]

time: 183 us -> 183 us (level)
  no operation moved by 1% of the time
where the time goes in v5:
time: 183 us
  Pallas kernels  51.5 us (28%)
  waiting for transfers between devices  46.6 us (25%)
  starting transfers between devices  45 us (25%)
  blocking collectives  35 us (19%)
  local copies, waits for them, and re-layouts  2.78 us (2%)
    ppermute x12, waiting for transfers between devices, along(): return lax.ppermute(part, 'pair', z_shift(ranks, step))  38.5 us
    all_to_all x1, blocking collectives, local(): both = exchange(jnp.broadcast_to(both[None], (owners, 2 * rows, columns)))  35 us
    pallas_call x2, Pallas kernels, half_ladder(): pl.pallas_call(functools.partial(half_kernel, first), grid=(1,), in_specs...  19.8 us
    pallas_call x1, Pallas kernels, update_main(): pl.pallas_call(main_kernel, grid_spec=grid_spec, out_shape=[jax.ShapeDtyp...  19.8 us
    ppermute x12, starting transfers between devices, along(): return lax.ppermute(part, 'pair', z_shift(ranks, step))  17.5 us
    ppermute x16, starting transfers between devices, across(): return [lax.ppermute(part, 'pair', other_core(ranks)) for part in parts]  11.8 us
    pallas_call x1, Pallas kernels, update_ladder(): pl.pallas_call(functools.partial(ladder_kernel, first, cuts), in_specs=[p...  9.59 us
    all_to_all x1, starting transfers between devices, local(): half_tail = exchange(sent)  5.87 us
  transfers between devices with their start and end apart: 31, of which 15 were waited for; matrix products, arithmetic and copies ran while one was open for 1% of the time, Pallas kernels for 22%

profile of v5, /device:TPU:1, one launch (start us, length us, event | category | flops | bytes accessed | tf_op | source)
XLA Modules:
  0.0 182.6 jit_solution(12132777432480900411)
XLA Ops:
  1.1 35.0 %all_to_all.20 = bf16[16,32,2048]{2,1,0:T(8,128)(2,1)S(1)} all-to-all(bf16[16,32,2048]{2,1,0:T(8,128)(2,1)S(1)} %broadcast_in_dim.4), channel_id=1, replica_groups=mesh['pair'=8,'virt'=16] {'virt'}, dimensions={0} | all-to-all | bytes 4194304 | tf_op jit(solution)/shard_map/spread_panels/all_to_all | solution.py:384
  36.5 2.2 %split_columns.1 = bf16[16,8,128,128]{3,2,1,0:T(8,128)(2,1)} custom-call(bf16[8,128,2048]{2,1,0:T(8,128)(2,1)S(1)} %copy-done), custom_call_target="tpu_custom_call" | custom-call | flops 1 | bytes 1 | tf_op jit(solution)/shard_map/exchange_amplitudes/split_columns/pallas_call | solution.py:78
  38.7 4.6 %all-to-all-start.1 = ((bf16[16,1024,128]{2,1,0:T(8,128)(2,1)}), bf16[16,1024,128]{2,1,0:T(8,128)(2,1)}, u32[]{:S(2)}, u32[]{:S(2)}) async-start(bf16[16,1024,128]{2,1,0:T(8,128)(2,1)} %bitcast.7), calls=%async_computation.1 | async-start | bytes 8388608 | tf_op jit(solution)/shard_map/exchange_amplitudes/all_to_all | solution.py:394
  43.3 2.1 %collective-permute-start.2 = (bf16[128,2048]{1,0:T(8,128)(2,1)S(1)}, bf16[128,2048]{1,0:T(8,128)(2,1)S(1)}, u32[]{:S(2)}, u32[]{:S(2)}) collective-permute-start(bf16[128,2048]{1,0:T(8,128)(2,1)S(1)} %bitcast.23), channel_id=1, source_target_pairs={{0,16},{16,0},{32,48},{48,32},{64,80},{80,64},{96,112},{112,96},{1... | collective-permute-start | bytes 1572872 | tf_op jit(solution)/shard_map/gather_ladder/ppermute | solution.py:374
  45.4 1.7 collective-permute-start
  47.4 1.9 %collective-permute-start.1 = (bf16[128,2048]{1,0:T(8,128)(2,1)S(1)}, bf16[128,2048]{1,0:T(8,128)(2,1)S(1)}, u32[]{:S(2)}, u32[]{:S(2)}) collective-permute-start(bf16[128,2048]{1,0:T(8,128)(2,1)S(1)} %bitcast.18), channel_id=1, source_target_pairs={{0,96},{16,112},{32,0},{48,16},{64,32},{80,48},{96,64},{112,80},{1... | collective-permute-start | bytes 1572872 | tf_op jit(solution)/shard_map/gather_ladder/ppermute | solution.py:371
  49.3 1.7 collective-permute-start.5
  51.0 10.4 %collective-permute-done.refs_2_.refs_18_ = bf16[128,2048]{1,0:T(8,128)(2,1)S(1)} collective-permute-done((bf16[128,2048]{1,0:T(8,128)(2,1)S(1)}, bf16[128,2048]{1,0:T(8,128)(2,1)S(1)}, u32[]{:S(2)}, u32[]{:S(2)}) %collective-permute-start) | collective-permute-done | bytes 524320 | tf_op jit(solution)/shard_map/gather_ladder/ppermute | solution.py:371
  62.5 1.7 collective-permute-start.7
  64.2 1.7 collective-permute-start.8
  65.9 6.6 %collective-permute-done.5.refs_5_.refs_21_ = bf16[128,2048]{1,0:T(8,128)(2,1)} collective-permute-done((bf16[128,2048]{1,0:T(8,128)(2,1)S(1)}, bf16[128,2048]{1,0:T(8,128)(2,1)}, u32[]{:S(2)}, u32[]{:S(2)}) %collective-permute-start.5) | collective-permute-done | bytes 524320 | tf_op jit(solution)/shard_map/gather_ladder/ppermute | solution.py:371
  73.6 10.3 %collective-permute-done.6.refs_6_.refs_22_ = bf16[128,2048]{1,0:T(8,128)(2,1)} collective-permute-done((bf16[128,2048]{1,0:T(8,128)(2,1)S(1)}, bf16[128,2048]{1,0:T(8,128)(2,1)}, u32[]{:S(2)}, u32[]{:S(2)}) %collective-permute-start.6) | collective-permute-done | bytes 524320 | tf_op jit(solution)/shard_map/gather_ladder/ppermute | solution.py:371
  87.4 2.3 %collective-permute-start.15 = (bf16[128,2048]{1,0:T(8,128)(2,1)S(1)}, bf16[128,2048]{1,0:T(8,128)(2,1)}, u32[]{:S(2)}, u32[]{:S(2)}) collective-permute-start(bf16[128,2048]{1,0:T(8,128)(2,1)S(1)} %bitcast.9), channel_id=1, source_target_pairs={{0,96},{16,112},{32,0},{48,16},{64,32},{80,48},{96,64},{112,80},{1... | collective-permute-start | bytes 1572872 | tf_op jit(solution)/shard_map/gather_cycle/ppermute | solution.py:371
  90.8 9.9 %half_ladder.2 = bf16[16,512,128]{2,1,0:T(8,128)(2,1)} custom-call(s32[1]{0:T(128)} %bitcast.place_ref, bf16[8,128,2048]{2,1,0:T(8,128)(2,1)} %a_ref.3, bf16[128,2048]{1,0:T(8,128)(2,1)} %bitcast.26, bf16[128,2048]{1,0:T(8,128)(2,1)} %bitcast.20, bf16[128,2048]{1,0:T(8,128)(2,1)} %copy-done.7, bf16[128,2048]{1,0:T(8,128)(2,1)} %copy-done.9, ...), custom_call_target="tpu_custom_call" | custom-call | flops 4294967296 | bytes 8388608 | tf_op jit(solution)/shard_map/half_ladder/half_ladder/pallas_call | solution.py:116
  102.7 5.2 %all-to-all-start.2 = ((bf16[16,512,128]{2,1,0:T(8,128)(2,1)}), bf16[16,512,128]{2,1,0:T(8,128)(2,1)S(1)}, u32[]{:S(2)}, u32[]{:S(2)}) async-start(bf16[16,512,128]{2,1,0:T(8,128)(2,1)} %half_ladder.2), calls=%async_computation.2 | async-start | bytes 4194304 | tf_op jit(solution)/shard_map/half_ladder/all_to_all | solution.py:413
  107.9 3.1 %collective-permute-start.17 = (bf16[128,2048]{1,0:T(8,128)(2,1)}, bf16[128,2048]{1,0:T(8,128)(2,1)S(1)}, u32[]{:S(2)}, u32[]{:S(2)}) collective-permute-start(bf16[128,2048]{1,0:T(8,128)(2,1)} %bitcast.14), channel_id=1, source_target_pairs={{0,96},{16,112},{32,0},{48,16},{64,32},{80,48},{96,64},{112,80},{1... | collective-permute-start | bytes 1572872 | tf_op jit(solution)/shard_map/gather_cycle/ppermute | solution.py:371
  111.0 2.7 %collective-permute-start.19 = (bf16[128,2048]{1,0:T(8,128)(2,1)}, bf16[128,2048]{1,0:T(8,128)(2,1)}, u32[]{:S(2)}, u32[]{:S(2)}) collective-permute-start(bf16[128,2048]{1,0:T(8,128)(2,1)} %collective-permute-done.15.refs_3_), channel_id=1, source_target_pairs={{0,96},{16,112},{32,0},{48,16},{64,32},{80,48},{96,64},{112,80},{1... | collective-permute-start | bytes 1572872 | tf_op jit(solution)/shard_map/gather_cycle/ppermute | solution.py:371
  113.7 9.9 %half_ladder.3 = bf16[16,512,128]{2,1,0:T(8,128)(2,1)} custom-call(s32[1]{0:T(128)} %bitcast.place_ref, bf16[8,128,2048]{2,1,0:T(8,128)(2,1)} %a_ref.3, bf16[128,2048]{1,0:T(8,128)(2,1)} %bitcast.27, bf16[128,2048]{1,0:T(8,128)(2,1)} %bitcast.21, bf16[128,2048]{1,0:T(8,128)(2,1)} %copy-done.7, bf16[128,2048]{1,0:T(8,128)(2,1)} %copy-done.9, ...), custom_call_target="tpu_custom_call" | custom-call | flops 4294967296 | bytes 8388608 | tf_op jit(solution)/shard_map/half_ladder/half_ladder/pallas_call | solution.py:116
  123.7 10.8 %collective-permute-done.18.refs_6_ = bf16[128,2048]{1,0:T(8,128)(2,1)} collective-permute-done((bf16[128,2048]{1,0:T(8,128)(2,1)}, bf16[128,2048]{1,0:T(8,128)(2,1)}, u32[]{:S(2)}, u32[]{:S(2)}) %collective-permute-start.18) | collective-permute-done | bytes 524320 | tf_op jit(solution)/shard_map/gather_cycle/ppermute | solution.py:371
  134.4 1.7 all-to-all-done.2.h_ref
  136.1 5.9 %all-to-all-start.3 = ((bf16[16,512,128]{2,1,0:T(8,128)(2,1)}), bf16[16,512,128]{2,1,0:T(8,128)(2,1)}, u32[]{:S(2)}, u32[]{:S(2)}) async-start(bf16[16,512,128]{2,1,0:T(8,128)(2,1)} %half_ladder.3), calls=%async_computation.3 | async-start | bytes 4194304 | tf_op jit(solution)/shard_map/half_ladder/all_to_all | solution.py:420
  142.0 3.1 %collective-permute-start.20 = (bf16[128,2048]{1,0:T(8,128)(2,1)}, bf16[128,2048]{1,0:T(8,128)(2,1)S(1)}, u32[]{:S(2)}, u32[]{:S(2)}) collective-permute-start(bf16[128,2048]{1,0:T(8,128)(2,1)} %bitcast.15), channel_id=1, source_target_pairs={{0,16},{16,0},{32,48},{48,32},{64,80},{80,64},{96,112},{112,96},{1... | collective-permute-start | bytes 1572872 | tf_op jit(solution)/shard_map/gather_cycle/ppermute | solution.py:374
  153.0 19.8 %update_main.1 = (bf16[8,2048,128]{2,1,0:T(8,128)(2,1)}, f32[2,2048,256]{2,1,0:T(8,128)}, bf16[8,256,2048]{2,1,0:T(8,128)(2,1)}) custom-call(s32[1]{0:T(128)} %bitcast.place_ref, f32[8]{0:T(128)S(1)} %copy-done.1, bf16[16,1024,128]{2,1,0:T(8,128)(2,1)} %all-to-all-done.1.a_ref, bf16[16,512,128]{2,1,0:T(8,128)(2,1)S(1)} %all-to-all-done.2.h_ref, ...), custom_call_target="tpu_custom_call" | custom-call | flops 1 | bytes 1 | tf_op jit(solution)/shard_map/update/update_main/pallas_call | solution.py:301
  172.8 9.6 %update_ladder.1 = bf16[8,2048,128]{2,1,0:T(8,128)(2,1)} custom-call(f32[8]{0:T(128)S(1)} %copy-done.1, bf16[2048,2048]{1,0:T(8,128)(2,1)} %bitcast.8, bf16[16,512,128]{2,1,0:T(8,128)(2,1)} %all-to-all-done.3.h_ref, f32[2,2048,256]{2,1,0:T(8,128)} %get-tuple-element.67.part_hbm, ...), custom_call_target="tpu_custom_call", output_to_operand_aliasing={{}: (6, {})} | custom-call | flops 1 | bytes 1 | tf_op jit(solution)/shard_map/update/update_ladder/pallas_call | solution.py:326
  (103 shorter events, 18.3 us)
Async XLA Ops:
  38.7 64.0 %all-to-all-start.1 = ((bf16[16,1024,128]{2,1,0:T(8,128)(2,1)}), bf16[16,1024,128]{2,1,0:T(8,128)(2,1)}, u32[]{:S(2)}, u32[]{:S(2)}) async-start(bf16[16,1024,128]{2,1,0:T(8,128)(2,1)} %bitcast.7), calls=%async_computation.1 | async-start | bytes 8388608 | tf_op jit(solution)/shard_map/exchange_amplitudes/all_to_all | solution.py:394
  43.3 7.7 %collective-permute-start.2 = (bf16[128,2048]{1,0:T(8,128)(2,1)S(1)}, bf16[128,2048]{1,0:T(8,128)(2,1)S(1)}, u32[]{:S(2)}, u32[]{:S(2)}) collective-permute-start(bf16[128,2048]{1,0:T(8,128)(2,1)S(1)} %bitcast.23), channel_id=1, source_target_pairs={{0,16},{16,0},{32,48},{48,32},{64,80},{80,64},{96,112},{112,96},{1... | collective-permute-start | bytes 1572872 | tf_op jit(solution)/shard_map/gather_ladder/ppermute | solution.py:374
  45.4 16.1 %collective-permute-start = (bf16[128,2048]{1,0:T(8,128)(2,1)S(1)}, bf16[128,2048]{1,0:T(8,128)(2,1)S(1)}, u32[]{:S(2)}, u32[]{:S(2)}) collective-permute-start(bf16[128,2048]{1,0:T(8,128)(2,1)S(1)} %bitcast.24), channel_id=1, source_target_pairs={{0,32},{16,48},{32,64},{48,80},{64,96},{80,112},{96,0},{112,16},{1... | collective-permute-start | bytes 1572872 | tf_op jit(solution)/shard_map/gather_ladder/ppermute | solution.py:371
  47.0 14.4 %collective-permute-start.3 = (bf16[128,2048]{1,0:T(8,128)(2,1)S(1)}, bf16[128,2048]{1,0:T(8,128)(2,1)S(1)}, u32[]{:S(2)}, u32[]{:S(2)}) collective-permute-start(bf16[128,2048]{1,0:T(8,128)(2,1)S(1)} %bitcast.17), channel_id=1, source_target_pairs={{0,16},{16,0},{32,48},{48,32},{64,80},{80,64},{96,112},{112,96},{1... | collective-permute-start | bytes 1572872 | tf_op jit(solution)/shard_map/gather_ladder/ppermute | solution.py:374
  47.4 14.1 %collective-permute-start.1 = (bf16[128,2048]{1,0:T(8,128)(2,1)S(1)}, bf16[128,2048]{1,0:T(8,128)(2,1)S(1)}, u32[]{:S(2)}, u32[]{:S(2)}) collective-permute-start(bf16[128,2048]{1,0:T(8,128)(2,1)S(1)} %bitcast.18), channel_id=1, source_target_pairs={{0,96},{16,112},{32,0},{48,16},{64,32},{80,48},{96,64},{112,80},{1... | collective-permute-start | bytes 1572872 | tf_op jit(solution)/shard_map/gather_ladder/ppermute | solution.py:371
  49.3 23.2 %collective-permute-start.5 = (bf16[128,2048]{1,0:T(8,128)(2,1)S(1)}, bf16[128,2048]{1,0:T(8,128)(2,1)}, u32[]{:S(2)}, u32[]{:S(2)}) collective-permute-start(bf16[128,2048]{1,0:T(8,128)(2,1)S(1)} %bitcast.25), channel_id=1, source_target_pairs={{0,96},{16,112},{32,0},{48,16},{64,32},{80,48},{96,64},{112,80},{1... | collective-permute-start | bytes 1572872 | tf_op jit(solution)/shard_map/gather_ladder/ppermute | solution.py:371
  51.0 22.6 %collective-permute-start.4 = (bf16[128,2048]{1,0:T(8,128)(2,1)S(1)}, bf16[128,2048]{1,0:T(8,128)(2,1)S(1)}, u32[]{:S(2)}, u32[]{:S(2)}) collective-permute-start(bf16[128,2048]{1,0:T(8,128)(2,1)S(1)} %bitcast.19), channel_id=1, source_target_pairs={{0,32},{16,48},{32,64},{48,80},{64,96},{80,112},{96,0},{112,16},{1... | collective-permute-start | bytes 1572872 | tf_op jit(solution)/shard_map/gather_ladder/ppermute | solution.py:371
  61.5 22.4 %collective-permute-start.6 = (bf16[128,2048]{1,0:T(8,128)(2,1)S(1)}, bf16[128,2048]{1,0:T(8,128)(2,1)}, u32[]{:S(2)}, u32[]{:S(2)}) collective-permute-start(bf16[128,2048]{1,0:T(8,128)(2,1)S(1)} %collective-permute-done.refs_2_.refs_18_), channel_id=1, source_target_pairs={{0,32},{16,48},{32,64},{48,80},{64,96},{80,112},{96,0},{112,16},{1... | collective-permute-start | bytes 1572872 | tf_op jit(solution)/shard_map/gather_ladder/ppermute | solution.py:371
  62.5 21.4 %collective-permute-start.7 = (bf16[128,2048]{1,0:T(8,128)(2,1)S(1)}, bf16[128,2048]{1,0:T(8,128)(2,1)}, u32[]{:S(2)}, u32[]{:S(2)}) collective-permute-start(bf16[128,2048]{1,0:T(8,128)(2,1)S(1)} %collective-permute-done.1.refs_3_.refs_19_), channel_id=1, source_target_pairs={{0,96},{16,112},{32,0},{48,16},{64,32},{80,48},{96,64},{112,80},{1... | collective-permute-start | bytes 1572872 | tf_op jit(solution)/shard_map/gather_ladder/ppermute | solution.py:371
  64.2 20.9 %collective-permute-start.8 = (bf16[128,2048]{1,0:T(8,128)(2,1)S(1)}, bf16[128,2048]{1,0:T(8,128)(2,1)S(1)}, u32[]{:S(2)}, u32[]{:S(2)}) collective-permute-start(bf16[128,2048]{1,0:T(8,128)(2,1)S(1)} %collective-permute-done.refs_2_.refs_18_), channel_id=1, source_target_pairs={{0,16},{16,0},{32,48},{48,32},{64,80},{80,64},{96,112},{112,96},{1... | collective-permute-start | bytes 1572872 | tf_op jit(solution)/shard_map/gather_ladder/ppermute | solution.py:374
  72.5 13.5 %collective-permute-start.9 = (bf16[128,2048]{1,0:T(8,128)(2,1)S(1)}, bf16[128,2048]{1,0:T(8,128)(2,1)S(1)}, u32[]{:S(2)}, u32[]{:S(2)}) collective-permute-start(bf16[128,2048]{1,0:T(8,128)(2,1)S(1)} %collective-permute-done.1.refs_3_.refs_19_), channel_id=1, source_target_pairs={{0,16},{16,0},{32,48},{48,32},{64,80},{80,64},{96,112},{112,96},{1... | collective-permute-start | bytes 1572872 | tf_op jit(solution)/shard_map/gather_ladder/ppermute | solution.py:374
  84.6 6.2 %collective-permute-start.11 = (bf16[128,2048]{1,0:T(8,128)(2,1)}, bf16[128,2048]{1,0:T(8,128)(2,1)}, u32[]{:S(2)}, u32[]{:S(2)}) collective-permute-start(bf16[128,2048]{1,0:T(8,128)(2,1)} %collective-permute-done.5.refs_5_.refs_21_), channel_id=1, source_target_pairs={{0,16},{16,0},{32,48},{48,32},{64,80},{80,64},{96,112},{112,96},{1... | collective-permute-start | bytes 1572872 | tf_op jit(solution)/shard_map/gather_ladder/ppermute | solution.py:374
  84.7 6.1 %collective-permute-start.12 = (bf16[128,2048]{1,0:T(8,128)(2,1)}, bf16[128,2048]{1,0:T(8,128)(2,1)}, u32[]{:S(2)}, u32[]{:S(2)}) collective-permute-start(bf16[128,2048]{1,0:T(8,128)(2,1)} %collective-permute-done.6.refs_6_.refs_22_), channel_id=1, source_target_pairs={{0,16},{16,0},{32,48},{48,32},{64,80},{80,64},{96,112},{112,96},{1... | collective-permute-start | bytes 1572872 | tf_op jit(solution)/shard_map/gather_ladder/ppermute | solution.py:374
  85.1 5.7 %collective-permute-start.13 = (bf16[128,2048]{1,0:T(8,128)(2,1)}, bf16[128,2048]{1,0:T(8,128)(2,1)}, u32[]{:S(2)}, u32[]{:S(2)}) collective-permute-start(bf16[128,2048]{1,0:T(8,128)(2,1)} %collective-permute-done.7.refs_7_.refs_23_), channel_id=1, source_target_pairs={{0,16},{16,0},{32,48},{48,32},{64,80},{80,64},{96,112},{112,96},{1... | collective-permute-start | bytes 1572872 | tf_op jit(solution)/shard_map/gather_ladder/ppermute | solution.py:374
  86.0 15.2 %collective-permute-start.14 = (bf16[128,2048]{1,0:T(8,128)(2,1)S(1)}, bf16[128,2048]{1,0:T(8,128)(2,1)}, u32[]{:S(2)}, u32[]{:S(2)}) collective-permute-start(bf16[128,2048]{1,0:T(8,128)(2,1)S(1)} %bitcast.13), channel_id=1, source_target_pairs={{0,32},{16,48},{32,64},{48,80},{64,96},{80,112},{96,0},{112,16},{1... | collective-permute-start | bytes 1572872 | tf_op jit(solution)/shard_map/gather_cycle/ppermute | solution.py:371
  87.4 13.8 %collective-permute-start.15 = (bf16[128,2048]{1,0:T(8,128)(2,1)S(1)}, bf16[128,2048]{1,0:T(8,128)(2,1)}, u32[]{:S(2)}, u32[]{:S(2)}) collective-permute-start(bf16[128,2048]{1,0:T(8,128)(2,1)S(1)} %bitcast.9), channel_id=1, source_target_pairs={{0,96},{16,112},{32,0},{48,16},{64,32},{80,48},{96,64},{112,80},{1... | collective-permute-start | bytes 1572872 | tf_op jit(solution)/shard_map/gather_cycle/ppermute | solution.py:371
  102.7 33.4 %all-to-all-start.2 = ((bf16[16,512,128]{2,1,0:T(8,128)(2,1)}), bf16[16,512,128]{2,1,0:T(8,128)(2,1)S(1)}, u32[]{:S(2)}, u32[]{:S(2)}) async-start(bf16[16,512,128]{2,1,0:T(8,128)(2,1)} %half_ladder.2), calls=%async_computation.2 | async-start | bytes 4194304 | tf_op jit(solution)/shard_map/half_ladder/all_to_all | solution.py:413
  107.9 15.7 %collective-permute-start.17 = (bf16[128,2048]{1,0:T(8,128)(2,1)}, bf16[128,2048]{1,0:T(8,128)(2,1)S(1)}, u32[]{:S(2)}, u32[]{:S(2)}) collective-permute-start(bf16[128,2048]{1,0:T(8,128)(2,1)} %bitcast.14), channel_id=1, source_target_pairs={{0,96},{16,112},{32,0},{48,16},{64,32},{80,48},{96,64},{112,80},{1... | collective-permute-start | bytes 1572872 | tf_op jit(solution)/shard_map/gather_cycle/ppermute | solution.py:371
  111.0 12.7 %collective-permute-start.16 = (bf16[128,2048]{1,0:T(8,128)(2,1)}, bf16[128,2048]{1,0:T(8,128)(2,1)}, u32[]{:S(2)}, u32[]{:S(2)}) collective-permute-start(bf16[128,2048]{1,0:T(8,128)(2,1)} %bitcast.10), channel_id=1, source_target_pairs={{0,32},{16,48},{32,64},{48,80},{64,96},{80,112},{96,0},{112,16},{1... | collective-permute-start | bytes 1572872 | tf_op jit(solution)/shard_map/gather_cycle/ppermute | solution.py:371
  111.0 23.4 %collective-permute-start.18 = (bf16[128,2048]{1,0:T(8,128)(2,1)}, bf16[128,2048]{1,0:T(8,128)(2,1)}, u32[]{:S(2)}, u32[]{:S(2)}) collective-permute-start(bf16[128,2048]{1,0:T(8,128)(2,1)} %collective-permute-done.14.refs_2_), channel_id=1, source_target_pairs={{0,32},{16,48},{32,64},{48,80},{64,96},{80,112},{96,0},{112,16},{1... | collective-permute-start | bytes 1572872 | tf_op jit(solution)/shard_map/gather_cycle/ppermute | solution.py:371
  111.0 23.4 %collective-permute-start.19 = (bf16[128,2048]{1,0:T(8,128)(2,1)}, bf16[128,2048]{1,0:T(8,128)(2,1)}, u32[]{:S(2)}, u32[]{:S(2)}) collective-permute-start(bf16[128,2048]{1,0:T(8,128)(2,1)} %collective-permute-done.15.refs_3_), channel_id=1, source_target_pairs={{0,96},{16,112},{32,0},{48,16},{64,32},{80,48},{96,64},{112,80},{1... | collective-permute-start | bytes 1572872 | tf_op jit(solution)/shard_map/gather_cycle/ppermute | solution.py:371
  136.1 36.7 %all-to-all-start.3 = ((bf16[16,512,128]{2,1,0:T(8,128)(2,1)}), bf16[16,512,128]{2,1,0:T(8,128)(2,1)}, u32[]{:S(2)}, u32[]{:S(2)}) async-start(bf16[16,512,128]{2,1,0:T(8,128)(2,1)} %half_ladder.3), calls=%async_computation.3 | async-start | bytes 4194304 | tf_op jit(solution)/shard_map/half_ladder/all_to_all | solution.py:420
  142.0 4.9 %collective-permute-start.20 = (bf16[128,2048]{1,0:T(8,128)(2,1)}, bf16[128,2048]{1,0:T(8,128)(2,1)S(1)}, u32[]{:S(2)}, u32[]{:S(2)}) collective-permute-start(bf16[128,2048]{1,0:T(8,128)(2,1)} %bitcast.15), channel_id=1, source_target_pairs={{0,16},{16,0},{32,48},{48,32},{64,80},{80,64},{96,112},{112,96},{1... | collective-permute-start | bytes 1572872 | tf_op jit(solution)/shard_map/gather_cycle/ppermute | solution.py:374
  145.7 4.1 %collective-permute-start.24 = (bf16[128,2048]{1,0:T(8,128)(2,1)}, bf16[128,2048]{1,0:T(8,128)(2,1)S(1)}, u32[]{:S(2)}, u32[]{:S(2)}) collective-permute-start(bf16[128,2048]{1,0:T(8,128)(2,1)} %collective-permute-done.16.refs_4_), channel_id=1, source_target_pairs={{0,16},{16,0},{32,48},{48,32},{64,80},{80,64},{96,112},{112,96},{1... | collective-permute-start | bytes 1572872 | tf_op jit(solution)/shard_map/gather_cycle/ppermute | solution.py:374
  (32 other events, 464.7 us)
